TPU v7x, 32 devices: a whole 2x2x4 slice. The times are simulated.
32 devices in a mesh: chan: 4 (over z), rad: 8 (over y, x, core).
Axes of the slice: x: 2, y: 2, z: 4, core: 2. Of those that a mesh axis runs over, the one named last changes fastest.
Arguments:
- vectors: float32 [1, 2, 104, 512, 512], P(None, None, 'chan', 'rad'), may hold values from -6 to 6
- eigenvectors: float32 [2, 512, 512], replicated, may hold values from -0.1875 to 0.1875
- energies: float32 [512], replicated, may hold values from 0 to 2
- widths: float32 [512], replicated, may hold values from 0 to 1
- shift_energy: float32 [1], replicated, may hold values from 0.5 to 2
- shift_width: float32 [1], replicated, may hold values from 0.5 to 1
- slot_channel: int32 [104], replicated, may hold values from 0 to 103, as said below
- partners: int32 [104, 12], replicated, may hold values from 0 to 103
- multipole: int32 [104, 12], replicated, may hold values from 0 to 3
- counts: int32 [104], replicated, may hold values from 1 to 12, as said below
- angular: float32 [104, 12], replicated, may hold values from -12 to 12
Outputs:
- update: float32 [1, 2, 104, 512, 512], P(None, None, 'chan', 'rad')
Inputs may be any that keep to these rules, and one draw needn't show every extreme that they name: `slot_channel`: a permutation of the channel numbers; slot s belongs to group s // 26. Entries at positions counts[c] and beyond of a channel's lists are ignored.
All inputs are finite; a program needn't handle non-finite values.
Results may differ from a plain program's by a relative error of at most 0.0024.
Values may be sent and summed in bfloat16 or wider, within the bound.
No kernel may reach another device: no remote copies, remote signals or barrier semaphores. Data moves between devices by JAX's collectives and lax.ppermute only.
A program may use at most 192 MiB of HBM per device.

v0:
```python
import functools

import jax
import jax.numpy as jnp
from jax import lax
from jax.experimental import pallas as pl
from jax.experimental.pallas import tpu as pltpu
from jax.sharding import PartitionSpec as P

ORDERS = 4
LANES = 128
GROUP_ROWS = 16

spacing = 0.01
first_point = 8.0
angle_ecs = 0.3

bf16 = jnp.bfloat16
f32 = jnp.float32
i16 = jnp.int16
i32 = jnp.int32
VMEM = pl.BlockSpec(memory_space=pltpu.VMEM)
SMEM = pl.BlockSpec(memory_space=pltpu.SMEM)
ANY = pl.BlockSpec(memory_space=pl.ANY)
ROOM = pltpu.CompilerParams(vmem_limit_bytes=60 << 20)
LEAN = pltpu.CompilerParams(vmem_limit_bytes=20 << 20)


def contour(index, points):
    start = 3 * points // 4
    position = spacing * (index.astype(f32) + first_point)
    edge = spacing * (start + first_point)
    beyond = jnp.maximum(position - edge, 0.0)
    return (jnp.minimum(position, edge) + beyond * jnp.cos(angle_ecs), beyond * jnp.sin(angle_ecs))


def complex_product(first, second):
    return (
        first[0] * second[0] - first[1] * second[1],
        first[0] * second[1] + first[1] * second[0],
    )


def coded_parts(parts):
    rows, points = parts[0].shape
    groups = rows // GROUP_ROWS
    codes, exponents = [], []
    for part in parts:
        top = jnp.abs(part[:, 0:LANES])
        for c in range(1, points // LANES):
            top = jnp.maximum(top, jnp.abs(part[:, c * LANES : (c + 1) * LANES]))
        top = jnp.max(top.reshape(groups, GROUP_ROWS, LANES), axis=1)
        top = jnp.maximum(jnp.max(top, axis=1, keepdims=True), 1e-30)
        exponent = jnp.broadcast_to(jnp.ceil(jnp.log2(top * 1.0001)), (groups, LANES))
        scale = jnp.exp2(15.0 - exponent)
        scale = jnp.broadcast_to(scale[:, None, :], (groups, GROUP_ROWS, LANES)).reshape(rows, LANES)
        codes.append(
            [
                jnp.round(part[:, c * LANES : (c + 1) * LANES] * scale).astype(i32).astype(i16)
                for c in range(points // LANES)
            ]
        )
        exponents.append(exponent)
    return codes, exponents


def tail_of(exponents):
    used = sum(e.shape[0] for e in exponents)
    rest = [jnp.zeros((GROUP_ROWS - used, LANES), f32)] if used < GROUP_ROWS else []
    return jnp.concatenate(exponents + rest, axis=0).astype(i32).astype(i16)


def decode_piece(load, rows, points, put):
    chunks = points // LANES
    groups = rows // GROUP_ROWS
    scales = jnp.exp2(load(2 * chunks * rows).astype(i32).astype(f32) - 15.0)
    for q in range(2):
        for g in range(groups):
            at = q * groups + g
            scale = scales[at : at + 1, :]
            for c in range(chunks):
                coded = load((q * chunks + c) * rows + g * GROUP_ROWS)
                put(q, g * GROUP_ROWS, c * LANES, coded.astype(i32).astype(f32) * scale)


def piece_rows(rows, points):
    return 2 * (points // LANES) * rows + GROUP_ROWS


def slot_to(spot, live):
    return spot & (live - 1) if live & (live - 1) == 0 else spot


def encode_kernel(rounds, natural, spot_ref, *refs):
    xs, outs = refs[: len(rounds)], refs[len(rounds) :]
    rad = outs[0].shape[0] if natural else 2 * len(outs)
    for j, (_, live) in enumerate(rounds):
        rows, points = xs[j].shape[3:]
        chunks = points // LANES
        size = piece_rows(rows, points)
        for d in range(rad):
            out_ref = outs[0].at[d] if natural else outs[d // 2]
            base = j * size if natural else ((d % 2) * len(rounds) + j) * size
            slot = slot_to(d if natural else spot_ref[0] ^ d, live)
            kept = jnp.where(slot < live, 1.0, 0.0)
            slot = jnp.minimum(slot, live - 1)
            codes, exponents = coded_parts([xs[j][0, q, slot] * kept for q in range(2)])
            for q in range(2):
                for c, code in enumerate(codes[q]):
                    out_ref[pl.ds(base + (q * chunks + c) * rows, rows), :] = code
            out_ref[pl.ds(base + size - GROUP_ROWS, GROUP_ROWS), :] = tail_of(exponents)


def encode_rounds(vectors, rounds, rad, spot, natural):
    _, _, group, rows, points = vectors.shape
    size = piece_rows(rows, points) * len(rounds)

    def block(start, live):
        return pl.BlockSpec((1, 2, live, rows, points), lambda i: (0, 0, start // live, 0, 0))

    if natural:
        shapes = [jax.ShapeDtypeStruct((rad, size, LANES), i16)]
    else:
        shapes = [jax.ShapeDtypeStruct((2 * size, LANES), i16)] * (rad // 2)
    return pl.pallas_call(
        functools.partial(encode_kernel, rounds, natural),
        grid=(1,),
        in_specs=[SMEM] + [block(*r) for r in rounds],
        out_specs=[VMEM] * len(shapes),
        out_shape=shapes,
        compiler_params=ROOM,
        cost_estimate=pl.CostEstimate(flops=0, bytes_accessed=6 * rad * size * LANES, transcendentals=0),
    )(spot, *[vectors for _ in rounds])


def halves_kernel(*refs):
    sources, out_ref, sems = refs[:-2], refs[-2], refs[-1]
    half = sources[0].shape[0] // 2
    copies = [
        pltpu.make_async_copy(ref.at[pl.ds(half, half)], out_ref.at[pl.ds(i * half, half)], sems.at[i])
        for i, ref in enumerate(sources)
    ]
    for copy in copies:
        copy.start()
    for copy in copies:
        copy.wait()


def second_halves(arrays):
    shape = arrays[0].shape
    return pl.pallas_call(
        halves_kernel,
        in_specs=[ANY] * len(arrays),
        out_specs=VMEM,
        out_shape=jax.ShapeDtypeStruct((len(arrays) * (shape[0] // 2),) + shape[1:], arrays[0].dtype),
        scratch_shapes=[pltpu.SemaphoreType.DMA((len(arrays),))],
        compiler_params=ROOM,
        cost_estimate=pl.CostEstimate(flops=0, bytes_accessed=4 << 20, transcendentals=0),
    )(*arrays)


class Pieces:
    def __init__(self, blocks, natural):
        self.blocks = blocks
        self.natural = natural

    def arrays(self):
        return [array for array, _ in self.blocks]

    def specs(self, lead):
        def spec(array, number):
            rest = array.shape[1:]
            return pl.BlockSpec((lead,) + rest, lambda i: (number,) + (0,) * len(rest))

        return [spec(array, number) for array, number in self.blocks]

    def views(self, refs, lead):
        return [ref.at[pl.ds(number * lead, lead)] for ref, (_, number) in zip(refs, self.blocks)]

    def place(self, at, me):
        return at if self.natural else me ^ at


def decode_kernel(live, rows, points, pieces, spot_ref, *refs):
    out_ref = refs[-1]
    for d, piece in enumerate(refs[:-2]):
        slot = slot_to(pieces.place(d, spot_ref[0]), live)

        def write():
            def put(q, row, column, value):
                out_ref[0, q, slot, pl.ds(row, GROUP_ROWS), pl.ds(column, LANES)] = value

            decode_piece(lambda row: piece[pl.ds(row, GROUP_ROWS), :], rows, points, put)

        if live & (live - 1) == 0:
            write()
        elif d < live:
            write()


def decode_round(pieces, total, start, live, spot, shape):
    _, _, _, rows, points = shape
    size = piece_rows(rows, points)
    count = len(pieces.blocks)
    aliases = {} if total is None else {1 + count: 0}
    return pl.pallas_call(
        functools.partial(decode_kernel, live, rows, points, pieces),
        grid=(1,),
        in_specs=[SMEM] + pieces.specs(size) + [ANY],
        out_specs=pl.BlockSpec((1, 2, live, rows, points), lambda i: (0, 0, start // live, 0, 0)),
        out_shape=jax.ShapeDtypeStruct(shape, f32),
        input_output_aliases=aliases,
        compiler_params=ROOM,
        cost_estimate=pl.CostEstimate(flops=0, bytes_accessed=6 * live * size * LANES, transcendentals=0),
    )(spot, *pieces.arrays(), spot if total is None else total)


def split(value):
    high = value.astype(bf16)
    return high, (value - high.astype(f32)).astype(bf16)


def dot(a, b):
    return jnp.dot(a, b, preferred_element_type=f32)


def dot_right(value, matrix, at):
    high, low = split(value)
    return dot(high, matrix[at]) + (dot(low, matrix[at]) + dot(high, matrix[at + 1]))


def dot_left(matrix, at, value):
    high, low = split(value)
    return dot(matrix[at], high) + (dot(matrix[at], low) + dot(matrix[at + 1], high))


def times_right(x, matrix, ready=(), finish=None):
    for copy in ready[:1]:
        copy.wait()
    k1 = dot_right(x[0] + x[1], matrix, 0)
    for copy in ready[1:2]:
        copy.wait()
    k3 = dot_right(x[1], matrix, 4)
    real = k1 - k3
    if finish is not None:
        finish(0, real)
    for copy in ready[2:]:
        copy.wait()
    k2 = dot_right(x[0], matrix, 2)
    if finish is not None:
        finish(1, k1 + k2)
    return real, k1 + k2


def times_left(matrix, x):
    k1 = dot_left(matrix, 0, x[0] + x[1])
    k2 = dot_left(matrix, 2, x[0])
    k3 = dot_left(matrix, 4, x[1])
    return k1 - k3, k1 + k2


class Copies:
    def __init__(self, sems):
        self.sems = sems
        self.count = 0

    def start(self, source, target):
        copy = pltpu.make_async_copy(source, target, self.sems.at[self.count])
        self.count += 1
        copy.start()
        return copy


def precondition(x_scr, given, held, copies, fill, finish, last=None):
    u_ref, ut_ref, factor_ref = held[:3]
    ready = [copies.start(given[0].at[pl.ds(at, 2)], u_ref.at[pl.ds(at, 2)]) for at in (0, 4, 2)]
    copy = copies.start(given[1], ut_ref)
    scaling = copies.start(given[2], factor_ref)
    fill()
    y = times_right((x_scr[0], x_scr[1]), u_ref, ready)
    copy.wait()
    y = times_left(ut_ref, y)
    scaling.wait()
    if last is not None:
        last()
    y = complex_product(y, (factor_ref[0], factor_ref[1]))
    y = times_left(u_ref, y)
    times_right(y, ut_ref, (), finish)


def p_scratch(points, count, pieces):
    matrix = pltpu.VMEM((6, points, points), bf16)
    field = pltpu.VMEM((2, points, points), f32)
    return [field, matrix, matrix] + [field] * (count - 2) + [pltpu.SemaphoreType.DMA((pieces + 8,))]


def prepare_kernel(shift_energy_ref, shift_width_ref, vec_ref, energy_ref, width_ref, u_ref, ut_ref, factor_ref):
    real, imag = vec_ref[0], vec_ref[1]
    for out, (r, i) in ((u_ref, (real, imag)), (ut_ref, (real.T, imag.T))):
        for at, value in enumerate((r, i - r, r + i)):
            high, low = split(value)
            out[2 * at] = high
            out[2 * at + 1] = low
    points = real.shape[0]

    def both(ref):
        column = jnp.broadcast_to(ref[...], (LANES, points)).T
        return jnp.concatenate([column] * (points // LANES), axis=1) + ref[...]

    den_real = both(energy_ref) - shift_energy_ref[0]
    den_imag = -both(width_ref) - shift_width_ref[0]
    modulus = den_real * den_real + den_imag * den_imag
    factor_ref[0] = den_real / modulus
    factor_ref[1] = -den_imag / modulus


def prepare(eigenvectors, energies, widths, shift_energy, shift_width):
    points = eigenvectors.shape[1]
    matrix = jax.ShapeDtypeStruct((6, points, points), bf16)
    return pl.pallas_call(
        prepare_kernel,
        in_specs=[SMEM] * 2 + [VMEM] * 3,
        out_specs=[VMEM] * 3,
        out_shape=[matrix, matrix, jax.ShapeDtypeStruct((2, points, points), f32)],
        compiler_params=ROOM,
        cost_estimate=pl.CostEstimate(flops=0, bytes_accessed=24 * points * points, transcendentals=0),
    )(shift_energy, shift_width, eigenvectors, energies[None, :], widths[None, :])


def p_cost(points):
    return pl.CostEstimate(flops=36 * 2 * points**3, bytes_accessed=16 * points * points, transcendentals=0)


def fill_from_rows(pieces, refs, x_scr, me, rows, points):
    for d, piece in enumerate(refs):
        base = pieces.place(d, me) * rows
        if not pieces.natural:
            base = pl.multiple_of(base, rows)

        def put(q, row, column, value):
            x_scr[q, pl.ds(base + row, GROUP_ROWS), pl.ds(column, LANES)] = value

        decode_piece(lambda row: piece[pl.ds(row, GROUP_ROWS), :], rows, points, put)


def first_kernel(plan, shared, pieces, spot_ref, *refs):
    rad, chan, rows, points, column_cuts, height = plan
    given, first_ref, outs = refs[rad : rad + 3], refs[rad + 3], refs[rad + 4 : -6]
    in_scr, x_scr, held, sems = refs[-6], refs[-5], refs[-4:-1], refs[-1]
    me, z_me = spot_ref[0], spot_ref[1]
    copies = Copies(sems)
    views = pieces.views(refs[:rad], piece_rows(rows, points))
    arriving = [copies.start(view, in_scr.at[p]) for p, view in enumerate(views)]
    leaving = []

    def fill():
        for copy in arriving:
            copy.wait()
        fill_from_rows(pieces, [in_scr.at[p] for p in range(rad)], x_scr, me, rows, points)

    def finish(q, value):
        x_scr[q] = value
        leaving.append(copies.start(x_scr.at[q], first_ref.at[q]))
        if shared is None:
            rounded = value.astype(bf16)
            for z in range(chan):
                column = (z % column_cuts) * LANES
                for p in range(rad):
                    row = p * rows + (z // column_cuts) * height
                    outs[0][z * rad + p, q] = rounded[row : row + height, column : column + LANES]
        else:
            for d in range(shared):
                row = pl.multiple_of((me ^ d) * rows, rows)
                for e in range(chan):
                    column = pl.multiple_of((z_me ^ e) * LANES, LANES)
                    outs[d][e, q] = x_scr[q, pl.ds(row, height), pl.ds(column, LANES)].astype(bf16)

    precondition(x_scr, given, held, copies, fill, finish)
    for copy in leaving:
        copy.wait()


def first_round(pieces, u, ut, factor, spot, plan, shared=None):
    rad, chan, rows, points, column_cuts, height = plan
    size = piece_rows(rows, points)
    if shared is None:
        sent = [jax.ShapeDtypeStruct((chan * rad, 2, height, LANES), bf16)]
    else:
        sent = [jax.ShapeDtypeStruct((chan, 2, height, LANES), bf16)] * shared
    result = pl.pallas_call(
        functools.partial(first_kernel, plan, shared, pieces),
        in_specs=[SMEM] + [ANY] * (rad + 3),
        out_specs=[ANY] + [VMEM] * len(sent),
        out_shape=[jax.ShapeDtypeStruct((2, points, points), f32)] + sent,
        scratch_shapes=[pltpu.VMEM((rad, size, LANES), i16)] + p_scratch(points, 3, rad),
        compiler_params=ROOM,
        cost_estimate=p_cost(points),
    )(spot, *pieces.arrays(), u, ut, factor)
    return result[0], result[1:]


def second_kernel(plan, shared, natural, pieces, spot_ref, *refs):
    rad, chan, rows, points, column_cuts, height = plan
    taken = 1 if shared is None else rad
    given, outs = refs[taken : taken + 4], refs[taken + 4 : -9]
    in_scr, code_scr, exp_scr, x_scr = refs[-9:-5]
    held, sems = refs[-5:-1], refs[-1]
    me, z_me = spot_ref[0], spot_ref[1]
    copies = Copies(sems)
    if shared is None:
        arriving = [copies.start(refs[0], in_scr)]
    else:
        views = pieces.views(refs[:rad], chan)
        arriving = [copies.start(view, in_scr.at[pl.ds(d * chan, chan)]) for d, view in enumerate(views)]
    groups = rows // GROUP_ROWS
    kept = []

    def fill():
        for copy in arriving:
            copy.wait()
        for q in range(2):
            if shared is None:
                for z in range(chan):
                    column = (z % column_cuts) * LANES
                    for p in range(rad):
                        row = p * rows + (z // column_cuts) * height
                        x_scr[q, pl.ds(row, height), pl.ds(column, LANES)] = in_scr[z * rad + p, q].astype(f32)
            else:
                for d in range(rad):
                    row = pl.multiple_of((me ^ d) * rows, rows)
                    for e in range(chan):
                        column = pl.multiple_of((z_me ^ e) * LANES, LANES)
                        x_scr[q, pl.ds(row, height), pl.ds(column, LANES)] = in_scr[d * chan + e, q].astype(f32)

    def last():
        kept.append(copies.start(given[3], held[3]))

    def finish(q, value):
        if q == 0:
            kept[0].wait()
        codes, exponents = coded_parts([held[3][q] - value])
        for c, code in enumerate(codes[0]):
            code_scr[q, c] = code
        for p in range(rad):
            exp_scr[p, pl.ds(q * groups, groups), :] = exponents[0][p * groups : (p + 1) * groups]

    precondition(x_scr, given, held, copies, fill, finish, last)
    chunks = points // LANES
    size = piece_rows(rows, points)
    for d in range(rad if shared is None else shared):
        spot = d if natural else me ^ d
        row = d * rows if natural else pl.multiple_of(spot * rows, rows)
        if natural:
            out_ref, base = outs[0], d * size
        elif shared is None:
            out_ref, base = outs[d // 2], (d % 2) * size
        else:
            out_ref, base = outs[d], 0
        for q in range(2):
            for c in range(chunks):
                out_ref[pl.ds(base + (q * chunks + c) * rows, rows), :] = code_scr[q, c, pl.ds(row, rows), :]
        out_ref[pl.ds(base + 2 * chunks * rows, GROUP_ROWS), :] = tail_of([exp_scr[spot]])


def tail_rows(rows):
    return 2 * (rows // GROUP_ROWS)


def second_round(pieces, first, u, ut, factor, spot, plan, shared=None, natural=False):
    rad, chan, rows, points, column_cuts, height = plan
    size = piece_rows(rows, points)
    if natural:
        shapes = [jax.ShapeDtypeStruct((rad * size, LANES), i16)]
    elif shared is None:
        shapes = [jax.ShapeDtypeStruct((2 * size, LANES), i16)] * (rad // 2)
    else:
        shapes = [jax.ShapeDtypeStruct((size, LANES), i16)] * shared
    given = [pieces] if shared is None else pieces.arrays()
    return pl.pallas_call(
        functools.partial(second_kernel, plan, shared, natural, pieces),
        in_specs=[SMEM] + [ANY] * (len(given) + 4),
        out_specs=[VMEM] * len(shapes),
        out_shape=shapes,
        scratch_shapes=[
            pltpu.VMEM((chan * rad, 2, height, LANES), bf16),
            pltpu.VMEM((2, points // LANES, points, LANES), i16),
            pltpu.VMEM((rad, tail_rows(rows), LANES), f32),
        ]
        + p_scratch(points, 4, len(given)),
        compiler_params=ROOM,
        cost_estimate=p_cost(points),
    )(spot, *given, u, ut, factor, first)


def weights_kernel(layout, channel_ref, partners_ref, multipole_ref, counts_ref, angular_ref, out_ref):
    chan, rad, full, live = layout
    links, channels = partners_ref.shape
    slots = out_ref.shape[1]
    group = channels // chan
    exact = dict(precision=lax.Precision.HIGHEST, preferred_element_type=f32)
    last = (((1,), (1,)), ((), ()))

    def ids(shape, axis):
        return lax.broadcasted_iota(i32, shape, axis)

    at, slot = ids((slots, channels), 0), ids((slots, channels), 1)
    z, inner = slot // group, slot % group
    found = (inner // rad) * (chan * rad) + z * rad + inner % rad
    if live:
        found = jnp.where(inner < full * rad, found, full * chan * rad + z * live + inner - full * rad)
    place = (at == found).astype(f32)
    held = (channel_ref[...] == ids((channels, channels), 0)).astype(f32)
    hot = lax.dot_general(place, held, last, **exact)
    tables = [jnp.zeros((channels, channels), f32) for _ in range(ORDERS)]
    for link in range(links):
        row = slice(link, link + 1)
        weight = jnp.where(counts_ref[...] > link, angular_ref[row, :], 0.0)
        spread = jnp.where(partners_ref[row, :] == ids((channels, channels), 0), weight, 0.0)
        for k in range(ORDERS):
            tables[k] = tables[k] + jnp.where(multipole_ref[row, :] == k, spread, 0.0)
    for k in range(ORDERS):
        targets = lax.dot_general(hot, tables[k], last, **exact)
        coupling = lax.dot_general(targets, hot, last, **exact)
        high, low = split(coupling)
        out_ref[k, :, 0:slots] = high
        out_ref[k, :, slots : 2 * slots] = low


def coupling_weights(slot_channel, partners, multipole, counts, angular, layout):
    chan, rad, full, live = layout
    slots = (full + (live > 0)) * chan * rad
    return pl.pallas_call(
        functools.partial(weights_kernel, layout),
        in_specs=[VMEM] * 5,
        out_specs=VMEM,
        out_shape=jax.ShapeDtypeStruct((ORDERS, slots, 2 * slots), bf16),
        compiler_params=ROOM,
        cost_estimate=pl.CostEstimate(flops=0, bytes_accessed=8 << 20, transcendentals=0),
    )(slot_channel[None, :], partners.T, multipole.T, counts[None, :], angular.T)


PACK = 4


def gather_kernel(shared, spot_ref, *refs):
    out_ref, scr = refs[-2], refs[-1]
    per = out_ref.shape[2]
    height = scr.shape[0] // per
    for q in range(2):
        if shared is None:
            for d in range(per):
                scr[pl.ds(d * height, height), :] = refs[0][d, q].astype(f32)
        else:
            scr[...] = jnp.zeros_like(scr)
            for e, ref in enumerate(refs[:-2]):
                for d in range(shared):
                    at = (spot_ref[1] ^ e) * shared + ((spot_ref[0] ^ d) & (shared - 1))
                    scr[pl.ds(pl.multiple_of(at * height, height), height), :] = ref[d, q].astype(f32)
        for r in range(height):
            value = scr[pl.ds(r, per, stride=height), :]
            out_ref[q, r // PACK, :, pl.ds((r % PACK) * LANES, LANES)] = value.astype(bf16)


def gather_round(pieces, spot, per, shared=None):
    height = pieces[0].shape[2]
    return pl.pallas_call(
        functools.partial(gather_kernel, shared),
        in_specs=[SMEM] + [VMEM] * len(pieces),
        out_specs=VMEM,
        out_shape=jax.ShapeDtypeStruct((2, height // PACK, per, PACK * LANES), bf16),
        scratch_shapes=[pltpu.VMEM((per * height, LANES), f32)],
        compiler_params=LEAN,
        cost_estimate=pl.CostEstimate(flops=0, bytes_accessed=8 * per * height * LANES, transcendentals=0),
    )(spot, *pieces)


def couple_kernel(sources, at, per, shared, spot_ref, weight_ref, table_ref, *refs):
    xs, scr = refs[:sources], refs[-1]
    outs = refs[sources:-1]
    packs = xs[0].shape[1]
    height = packs * PACK
    weight = weight_ref[:, at : at + per, :].reshape(ORDERS * per, weight_ref.shape[2])

    def step(g, carry):
        mixed = []
        for q in range(2):
            values = [x[q, g] for x in xs]
            mixed.append(dot(weight, jnp.concatenate(values + values, axis=0)))
        inverse = (table_ref[0, pl.ds(g, 1), :], table_ref[1, pl.ds(g, 1), :])
        ratio = (table_ref[2, pl.ds(g, 1), :], table_ref[3, pl.ds(g, 1), :])
        total = [mixed[q][(ORDERS - 1) * per :] for q in range(2)]
        for k in range(ORDERS - 2, -1, -1):
            total = complex_product(total, ratio)
            total = [total[q] + mixed[q][k * per : (k + 1) * per] for q in range(2)]
        total = complex_product(total, inverse)
        for q in range(2):
            for r in range(PACK):
                scr[q, pl.ds(g * PACK + r, per, stride=height), :] = total[q][:, r * LANES : (r + 1) * LANES]
        return carry

    lax.fori_loop(0, packs, step, 0, unroll=2)
    for q in range(2):
        if shared is None:
            for d in range(per):
                outs[0][d, q] = scr[q, pl.ds(d * height, height), :].astype(bf16)
        else:
            for e, out_ref in enumerate(outs):
                for d in range(shared):
                    slot = (spot_ref[1] ^ e) * shared + ((spot_ref[0] ^ d) & (shared - 1))
                    row = pl.multiple_of(slot * height, height)
                    out_ref[d, q] = scr[q, pl.ds(row, height), :].astype(bf16)


def couple_round(gathered, weights, table, spot, at, chan, per, shared=None):
    _, packs, _, width = gathered[0].shape
    height = packs * PACK
    slots = weights.shape[2]
    if shared is None:
        outs = [jax.ShapeDtypeStruct((per, 2, height, LANES), bf16)]
    else:
        outs = [jax.ShapeDtypeStruct((shared, 2, height, LANES), bf16)] * chan
    return pl.pallas_call(
        functools.partial(couple_kernel, len(gathered), at, per, shared),
        in_specs=[SMEM] + [VMEM] * (2 + len(gathered)),
        out_specs=[VMEM] * len(outs),
        out_shape=outs,
        scratch_shapes=[pltpu.VMEM((2, per * height, LANES), f32)],
        compiler_params=LEAN,
        cost_estimate=pl.CostEstimate(
            flops=32 * packs * per * slots * width, bytes_accessed=6 << 20, transcendentals=0
        ),
    )(spot, weights, table, *gathered)


def kernel_table(row_ids, col_ids, points):
    upper = contour(jnp.maximum(row_ids[:, None], col_ids[None, :]), points)
    lower = contour(jnp.minimum(row_ids[:, None], col_ids[None, :]), points)
    modulus = upper[0] * upper[0] + upper[1] * upper[1]
    inverse = (upper[0] / modulus, -upper[1] / modulus)
    ratio = complex_product(lower, inverse)
    return jnp.stack([inverse[0], inverse[1], ratio[0], ratio[1]])


def local(
    vectors,
    eigenvectors,
    energies,
    widths,
    shift_energy,
    shift_width,
    slot_channel,
    partners,
    multipole,
    counts,
    angular,
):
    _, _, group, rows, points = vectors.shape
    chan = lax.axis_size("chan")
    rad = lax.axis_size("rad")
    column_cuts = min(chan, points // LANES)
    height = rows // (chan // column_cuts)
    plan = (rad, chan, rows, points, column_cuts, height)
    full, live = group // rad, group % rad
    if live != 2 or column_cuts != chan:
        full, live = full + 1, 0
    spot = jnp.stack([lax.axis_index("rad"), lax.axis_index("chan")]).astype(i32)

    def over(piece, axis, size, d):
        return lax.ppermute(piece, axis, [(i, i ^ d) for i in range(size)])

    def over_even(arrays):
        return [arrays[0]] + [over(array, "rad", rad, 2 * e) for e, array in enumerate(arrays) if e]

    def over_next(got, count):
        half = got[0].shape[0] // 2
        swapped = over(second_halves(got), "rad", rad, 1)
        return [
            Pieces([(swapped, (d // 2) * count + j) if d % 2 else (got[d // 2], j) for d in range(rad)], False)
            for j in range(count)
        ]

    def over_chan(pieces):
        return [pieces[0]] + [over(piece, "chan", chan, e) for e, piece in enumerate(pieces) if e]

    def over_all(piece):
        return lax.all_to_all(piece, ("chan", "rad"), 0, 0, tiled=True)

    def share(piece):
        flat = lax.all_to_all(piece.reshape(rad, -1, LANES), "rad", 0, 0, tiled=True).reshape(-1, LANES)
        return Pieces([(flat, p) for p in range(rad)], True)

    rounds = [(j * rad, min(rad, group - j * rad)) for j in range(full)]
    if live:
        rounds.append((full * rad, live))
    everyone = chan * rad

    def cut(values):
        is_pieces = lambda v: isinstance(v, Pieces)
        leaves, tree = jax.tree.flatten(values, is_leaf=is_pieces)
        arrays = {}
        for leaf in leaves:
            for array in leaf.arrays() if is_pieces(leaf) else [leaf]:
                arrays[id(array)] = array
        tied = dict(zip(arrays, lax.optimization_barrier(list(arrays.values()))))
        leaves = [
            Pieces([(tied[id(array)], at) for array, at in leaf.blocks], leaf.natural)
            if is_pieces(leaf)
            else tied[id(leaf)]
            for leaf in leaves
        ]
        return jax.tree.unflatten(tree, leaves)

    near = [encode_rounds(vectors, [r], rad, spot, True)[0] for r in rounds[:2]]
    far = [encode_rounds(vectors, [r], rad, spot, False) for r in rounds[2:3]]
    u, ut, factor = prepare(eigenvectors, energies, widths, shift_energy, shift_width)
    small = (slot_channel, partners, multipole, counts, angular, spot)
    received, near, far, u, ut, factor, small, later = cut((share(near[0]), near, far, u, ut, factor, small, vectors))

    def apply_first(pieces, shared=None):
        return first_round(pieces, u, ut, factor, spot, plan, shared)

    def constants(small):
        weights = coupling_weights(*small[:5], (chan, rad, full, live))
        z = small[5][1]
        row_ids = small[5][0] * rows + (z // column_cuts) * height + jnp.arange(height, dtype=i32)
        col_ids = (z % column_cuts) * LANES + jnp.arange(LANES, dtype=i32)
        return weights, kernel_table(row_ids, col_ids, points).reshape(4, height // PACK, PACK * LANES)

    firsts, gathered, arriving, fixed = [], [], (), None
    first, pieces = apply_first(received)
    firsts.append(first)
    if len(near) > 1:
        received = share(near[1])
    flying, received, small, far, later = cut((pieces[0], received, small, far, later))
    for j in range(1, len(rounds)):
        flying = over_all(flying)
        if j > 1:
            received = over_next(arriving, 1)[0]
        arriving = over_even(far[j - 1]) if j - 1 < len(far) else ()
        if j == 1:
            far += [encode_rounds(later, [r], rad, spot, False) for r in rounds[3:]]
        if j == 2:
            fixed = constants(small)
        first, pieces = apply_first(received, live if j == full else None)
        firsts.append(first)
        if j == full:
            pieces = [pieces[0]] + [over(piece, "rad", rad, d) for d, piece in enumerate(pieces) if d]
            pieces = over_chan([jnp.stack([piece[e] for piece in pieces]) for e in range(chan)])
        flown, pieces, small, far, arriving, gathered, fixed = cut(
            (flying, pieces, small, far, arriving, gathered, fixed)
        )
        flying = pieces[0]
        gathered.append(gather_round([flown], spot, everyone))
    if not live:
        gathered.append(gather_round([over_all(flying)], spot, everyone))
    weights, table = fixed or constants(small)
    if live:
        gathered.append(gather_round(pieces, spot, everyone, live))

    def couple(j):
        if j == full:
            return couple_round(gathered, weights, table, spot, full * everyone, chan, chan * live, live)
        return couple_round(gathered, weights, table, spot, j * everyone, chan, everyone)[0]

    def apply_second(pieces, j, shared=None):
        return second_round(pieces, firsts[j], u, ut, factor, spot, plan, shared, shared is None and j >= full - 2)

    coupled, gathered, firsts = cut((couple(0), gathered, firsts))
    coupled = [coupled]
    update, shared, total, ready = None, None, None, []
    for j in range(full):
        flown = over_all(coupled[j])
        if j == 0:
            coupled += [couple(k) for k in range(1, full)]
            shared = over_chan(couple(full)) if live else None
        if live and j == min(1, full - 1):
            both = jnp.concatenate([jnp.stack([piece[d] for piece in shared]) for d in range(live)])
            shared = over_even([both] * (rad // 2))
        elif live and j == min(2, full - 1):
            shared = over_next(shared, 1)[0]
        if j > 2:
            ready[j - 3] = over_next(ready[j - 3], 1)[0]
        if update is not None:
            ready.append(over_even(update) if len(update) > 1 else update)
        update = apply_second(mine, j - 1) if j > 0 else None
        mine, coupled, update, ready, shared = cut((flown, coupled, update, ready, shared))
    ready = [over_next(got, 1)[0] if isinstance(got, list) else got for got in ready]
    if live and full < 3:
        shared = over_next(shared, 1)[0]
    if update is not None:
        ready.append(share(update[0]))
    update = apply_second(mine, full - 1)
    update, ready, shared = cut((update, ready, shared))
    done = share(update[0])
    for j, pieces in enumerate(ready):
        total = decode_round(pieces, total, *rounds[j], spot, vectors.shape)
    if live:
        extra = apply_second(shared, full, live)
        done, extra, total = cut((done, extra, total))
        extra = [extra[0]] + [over(piece, "rad", rad, d) for d, piece in enumerate(extra) if d]
        extra = Pieces([(piece, 0) for piece in extra], False)
    total = decode_round(done, total, *rounds[full - 1], spot, vectors.shape)
    if live:
        total = decode_round(extra, total, *rounds[full], spot, vectors.shape)
    return total


def solution(mesh):
    in_specs = (P(None, None, "chan", "rad", None),) + (P(),) * 10
    out_specs = P(None, None, "chan", "rad", None)
    return jax.shard_map(local, mesh=mesh, in_specs=in_specs, out_specs=out_specs, check_vma=False)
```

profile of v0, /device:TPU:1, one launch (start us, length us, event | category | flops | bytes accessed | tf_op | source)
XLA Modules:
  0.0 312.1 jit_solution(13988020440866226552)
XLA Ops:
  3.6 5.2 %all-to-all-start = ((s16[8,528,128]{2,1,0:T(8,128)(2,1)}), s16[8,528,128]{2,1,0:T(8,128)(2,1)S(1)}, u32[]{:S(2)}, u32[]{:S(2)}) async-start(s16[8,528,128]{2,1,0:T(8,128)(2,1)} %shard_map.109), calls=%async_computation | async-start | bytes 2162688 | tf_op jit(solution)/shard_map/all_to_all | solution.py:689
  16.2 5.8 %shard_map.112 = (bf16[6,512,512]{2,1,0:T(8,128)(2,1)}, bf16[6,512,512]{2,1,0:T(8,128)(2,1)}, f32[2,512,512]{2,1,0:T(8,128)}) custom-call(f32[1]{0:T(128)S(6)} %copy.25.shift_energy_ref, f32[1]{0:T(128)S(6)} %copy.26.shift_width_ref, f32[2,512,512]{2,1,0:T(8,128)} %vec_ref.1, f32[1,512]{1,0:T(1,128)} %bitcast.58, f32[1,512]{1,0:T(1,128)} %bitcast.59), custom_call_target="tpu_custom_call" | custom-call | bytes 6291456 | tf_op jit(solution)/shard_map/pallas_call | solution.py:320
  22.0 6.4 %all-to-all-start.1 = ((s16[8,528,128]{2,1,0:T(8,128)(2,1)}), s16[8,528,128]{2,1,0:T(8,128)(2,1)S(1)}, u32[]{:S(2)}, u32[]{:S(2)}) async-start(s16[8,528,128]{2,1,0:T(8,128)(2,1)} %shard_map.110), calls=%async_computation.1 | async-start | bytes 2162688 | tf_op jit(solution)/shard_map/all_to_all | solution.py:689
  28.4 15.2 %shard_map.113 = (f32[2,512,512]{2,1,0:T(8,128)}, bf16[32,2,64,128]{3,2,1,0:T(8,128)(2,1)}) custom-call(s32[2]{0:T(128)} %pad_add_fusion.spot_ref.refs_8_, s16[4224,128]{1,0:T(8,128)(2,1)} %bitcast.39, s16[4224,128]{1,0:T(8,128)(2,1)} %bitcast.40, s16[4224,128]{1,0:T(8,128)(2,1)} %bitcast.41, s16[4224,128]{1,0:T(8,128)(2,1)} %bitcast.42, ...), custom_call_target="tpu_custom_call" | custom-call | flops 9663676416 | bytes 4194304 | tf_op jit(solution)/shard_map/pallas_call | solution.py:390
  43.7 6.7 %all-to-all-start.2 = ((bf16[32,2,64,128]{3,2,1,0:T(8,128)(2,1)}), bf16[32,2,64,128]{3,2,1,0:T(8,128)(2,1)S(1)}, u32[]{:S(2)}, u32[]{:S(2)}) async-start(bf16[32,2,64,128]{3,2,1,0:T(8,128)(2,1)} %get-tuple-element.175), calls=%async_computation.2 | async-start | bytes 2097152 | tf_op jit(solution)/shard_map/all_to_all | solution.py:686
  53.2 15.2 %shard_map.114 = (f32[2,512,512]{2,1,0:T(8,128)}, bf16[32,2,64,128]{3,2,1,0:T(8,128)(2,1)}) custom-call(s32[2]{0:T(128)} %pad_add_fusion.spot_ref.refs_8_, s16[4224,128]{1,0:T(8,128)(2,1)} %bitcast.47, s16[4224,128]{1,0:T(8,128)(2,1)} %bitcast.48, s16[4224,128]{1,0:T(8,128)(2,1)} %bitcast.49, s16[4224,128]{1,0:T(8,128)(2,1)} %bitcast.50, ...), custom_call_target="tpu_custom_call" | custom-call | flops 9663676416 | bytes 4194304 | tf_op jit(solution)/shard_map/pallas_call | solution.py:390
  70.9 5.6 %collective-permute-done.2.refs_3_.refs_6_ = s16[1056,128]{1,0:T(8,128)(2,1)S(1)} collective-permute-done((s16[1056,128]{1,0:T(8,128)(2,1)S(1)}, s16[1056,128]{1,0:T(8,128)(2,1)S(1)}, u32[]{:S(2)}, u32[]{:S(2)}) %collective-permute-start.2) | collective-permute-done | bytes 270368 | tf_op jit(solution)/shard_map/ppermute | solution.py:669
  76.5 4.7 %all-to-all-start.3 = ((bf16[32,2,64,128]{3,2,1,0:T(8,128)(2,1)}), bf16[32,2,64,128]{3,2,1,0:T(8,128)(2,1)S(1)}, u32[]{:S(2)}, u32[]{:S(2)}) async-start(bf16[32,2,64,128]{3,2,1,0:T(8,128)(2,1)} %get-tuple-element.193), calls=%async_computation.3 | async-start | bytes 2097152 | tf_op jit(solution)/shard_map/all_to_all | solution.py:686
  95.8 15.3 %shard_map.117 = (f32[2,512,512]{2,1,0:T(8,128)}, bf16[32,2,64,128]{3,2,1,0:T(8,128)(2,1)}) custom-call(s32[2]{0:T(128)} %pad_add_fusion.spot_ref.refs_8_, s16[1056,128]{1,0:T(8,128)(2,1)} %get-tuple-element.194.refs_0_, s16[2112,128]{1,0:T(8,128)(2,1)} %collective-permute-done.3.refs_1_.refs_3_.refs_5_.refs_7_, s16[1056,128]{1,0:T(8,128)(2,1)} %copy-done.28, ...), custom_call_target="tpu_custom_call" | custom-call | flops 9663676416 | bytes 4194304 | tf_op jit(solution)/shard_map/pallas_call | solution.py:390
  113.1 6.6 %all-to-all-start.4 = ((bf16[32,2,64,128]{3,2,1,0:T(8,128)(2,1)}), bf16[32,2,64,128]{3,2,1,0:T(8,128)(2,1)}, u32[]{:S(2)}, u32[]{:S(2)}) async-start(bf16[32,2,64,128]{3,2,1,0:T(8,128)(2,1)} %get-tuple-element.210), calls=%async_computation.4 | async-start | bytes 2097152 | tf_op jit(solution)/shard_map/all_to_all | solution.py:686
  121.6 15.0 %shard_map.121 = (f32[2,512,512]{2,1,0:T(8,128)}, bf16[4,2,64,128]{3,2,1,0:T(8,128)(2,1)}, bf16[4,2,64,128]{3,2,1,0:T(8,128)(2,1)}) custom-call(s32[2]{0:T(128)} %pad_add_fusion.spot_ref.refs_8_, s16[1056,128]{1,0:T(8,128)(2,1)} %get-tuple-element.211.refs_0_, s16[2112,128]{1,0:T(8,128)(2,1)} %collective-permute-done.7.refs_1_.refs_3_.refs_5_.refs_7_, ...), custom_call_target="tpu_custom_call" | custom-call | flops 9663676416 | bytes 4194304 | tf_op jit(solution)/shard_map/pallas_call | solution.py:390
  143.3 5.8 %collective-permute-done.10.refs_2_ = bf16[2,2,64,128]{3,2,1,0:T(8,128)(2,1)S(1)} collective-permute-done((bf16[2,2,64,128]{3,2,1,0:T(8,128)(2,1)S(1)}, bf16[2,2,64,128]{3,2,1,0:T(8,128)(2,1)S(1)}, u32[]{:S(2)}, u32[]{:S(2)}) %collective-permute-start.10) | collective-permute-done | bytes 65568 | tf_op jit(solution)/shard_map/ppermute | solution.py:669
  155.2 4.9 %shard_map.125 = bf16[32,2,64,128]{3,2,1,0:T(8,128)(2,1)S(1)} custom-call(s32[2]{0:T(128)S(1)} %copy-done.8, bf16[4,128,256]{2,1,0:T(8,128)(2,1)S(1)} %copy-done.2, f32[4,16,512]{2,1,0:T(8,128)S(1)} %pad_maximum_fusion.table_ref, bf16[2,16,32,512]{3,2,1,0:T(8,128)(2,1)S(1)} %shard_map.118.refs_0_, bf16[2,16,32,512]{3,2,1,0:T(8,128)(2,1)S(1)} %shard_map.122.refs_1_, ...), custom_call_target="tpu_custom_call" | custom-call | flops 2147483648 | bytes 6291456 | tf_op jit(solution)/shard_map/pallas_call | solution.py:622
  173.6 5.9 %shard_map.127 = bf16[32,2,64,128]{3,2,1,0:T(8,128)(2,1)} custom-call(s32[2]{0:T(128)S(1)} %copy-done.8, bf16[4,128,256]{2,1,0:T(8,128)(2,1)S(1)} %copy-done.2, f32[4,16,512]{2,1,0:T(8,128)S(1)} %pad_maximum_fusion.table_ref, bf16[2,16,32,512]{3,2,1,0:T(8,128)(2,1)S(1)} %shard_map.118.refs_0_, bf16[2,16,32,512]{3,2,1,0:T(8,128)(2,1)S(1)} %shard_map.122.refs_1_, ...), custom_call_target="tpu_custom_call" | custom-call | flops 2147483648 | bytes 6291456 | tf_op jit(solution)/shard_map/pallas_call | solution.py:622
  179.5 4.9 %shard_map.126 = bf16[32,2,64,128]{3,2,1,0:T(8,128)(2,1)S(1)} custom-call(s32[2]{0:T(128)S(1)} %copy-done.8, bf16[4,128,256]{2,1,0:T(8,128)(2,1)S(1)} %copy-done.2, f32[4,16,512]{2,1,0:T(8,128)S(1)} %pad_maximum_fusion.table_ref, bf16[2,16,32,512]{3,2,1,0:T(8,128)(2,1)S(1)} %shard_map.118.refs_0_, bf16[2,16,32,512]{3,2,1,0:T(8,128)(2,1)S(1)} %shard_map.122.refs_1_, ...), custom_call_target="tpu_custom_call" | custom-call | flops 2147483648 | bytes 6291456 | tf_op jit(solution)/shard_map/pallas_call | solution.py:622
  185.4 9.9 %collective-permute-done.13 = bf16[2,2,64,128]{3,2,1,0:T(8,128)(2,1)S(1)} collective-permute-done((bf16[2,2,64,128]{3,2,1,0:T(8,128)(2,1)S(1)}, bf16[2,2,64,128]{3,2,1,0:T(8,128)(2,1)S(1)}, u32[]{:S(2)}, u32[]{:S(2)}) %collective-permute-start.13) | collective-permute-done | bytes 65568 | tf_op jit(solution)/shard_map/ppermute | solution.py:669
  204.6 14.7 %shard_map.129 = (s16[1056,128]{1,0:T(8,128)(2,1)}, s16[1056,128]{1,0:T(8,128)(2,1)}, s16[1056,128]{1,0:T(8,128)(2,1)}, s16[1056,128]{1,0:T(8,128)(2,1)}) custom-call(s32[2]{0:T(128)} %pad_add_fusion.spot_ref.refs_8_, bf16[32,2,64,128]{3,2,1,0:T(8,128)(2,1)} %all-to-all-done.5.refs_0_, bf16[6,512,512]{2,1,0:T(8,128)(2,1)} %get-tuple-element.159.refs_8_.refs_1_, ...), custom_call_target="tpu_custom_call" | custom-call | flops 9663676416 | bytes 4194304 | tf_op jit(solution)/shard_map/pallas_call | solution.py:479
  219.3 5.5 %collective-permute-done.16.refs_2_.refs_4_ = bf16[8,2,64,128]{3,2,1,0:T(8,128)(2,1)S(1)} collective-permute-done((bf16[8,2,64,128]{3,2,1,0:T(8,128)(2,1)S(1)}, bf16[8,2,64,128]{3,2,1,0:T(8,128)(2,1)S(1)}, u32[]{:S(2)}, u32[]{:S(2)}) %collective-permute-start.16) | collective-permute-done | bytes 262176 | tf_op jit(solution)/shard_map/ppermute | solution.py:669
  225.6 6.2 %all-to-all-start.7 = ((bf16[32,2,64,128]{3,2,1,0:T(8,128)(2,1)}), bf16[32,2,64,128]{3,2,1,0:T(8,128)(2,1)S(1)}, u32[]{:S(2)}, u32[]{:S(2)}) async-start(bf16[32,2,64,128]{3,2,1,0:T(8,128)(2,1)} %shard_map.127), calls=%async_computation.7 | async-start | bytes 2097152 | tf_op jit(solution)/shard_map/all_to_all | solution.py:686
  237.6 14.8 %shard_map.130 = s16[4224,128]{1,0:T(8,128)(2,1)} custom-call(s32[2]{0:T(128)} %pad_add_fusion.spot_ref.refs_8_, bf16[32,2,64,128]{3,2,1,0:T(8,128)(2,1)} %copy-done.25, bf16[6,512,512]{2,1,0:T(8,128)(2,1)} %get-tuple-element.159.refs_8_.refs_1_, bf16[6,512,512]{2,1,0:T(8,128)(2,1)} %get-tuple-element.160.refs_9_.refs_2_, ...), custom_call_target="tpu_custom_call" | custom-call | flops 9663676416 | bytes 4194304 | tf_op jit(solution)/shard_map/pallas_call | solution.py:479
  252.4 5.5 %collective-permute-done.20.refs_3_.refs_6_ = s16[1056,128]{1,0:T(8,128)(2,1)S(1)} collective-permute-done((s16[1056,128]{1,0:T(8,128)(2,1)}, s16[1056,128]{1,0:T(8,128)(2,1)S(1)}, u32[]{:S(2)}, u32[]{:S(2)}) %collective-permute-start.20) | collective-permute-done | bytes 270368 | tf_op jit(solution)/shard_map/ppermute | solution.py:669
  258.9 4.8 %all-to-all-start.8 = ((s16[8,528,128]{2,1,0:T(8,128)(2,1)}), s16[8,528,128]{2,1,0:T(8,128)(2,1)S(1)}, u32[]{:S(2)}, u32[]{:S(2)}) async-start(s16[8,528,128]{2,1,0:T(8,128)(2,1)} %bitcast.37), calls=%async_computation.8 | async-start | bytes 2162688 | tf_op jit(solution)/shard_map/all_to_all | solution.py:689
  265.9 14.8 %shard_map.132 = s16[4224,128]{1,0:T(8,128)(2,1)} custom-call(s32[2]{0:T(128)} %pad_add_fusion.spot_ref.refs_8_, bf16[32,2,64,128]{3,2,1,0:T(8,128)(2,1)} %copy-done.26, bf16[6,512,512]{2,1,0:T(8,128)(2,1)} %get-tuple-element.159.refs_8_.refs_1_, bf16[6,512,512]{2,1,0:T(8,128)(2,1)} %get-tuple-element.160.refs_9_.refs_2_, ...), custom_call_target="tpu_custom_call" | custom-call | flops 9663676416 | bytes 4194304 | tf_op jit(solution)/shard_map/pallas_call | solution.py:479
  291.0 14.6 %shard_map.134 = (s16[528,128]{1,0:T(8,128)(2,1)}, s16[528,128]{1,0:T(8,128)(2,1)}) custom-call(s32[2]{0:T(128)} %pad_add_fusion.spot_ref.refs_8_, bf16[8,2,64,128]{3,2,1,0:T(8,128)(2,1)} %copy-done.27, bf16[16,2,64,128]{3,2,1,0:T(8,128)(2,1)} %copy-done.38, bf16[8,2,64,128]{3,2,1,0:T(8,128)(2,1)} %collective-permute-done.15.refs_1_.refs_2_, ...), custom_call_target="tpu_custom_call" | custom-call | flops 9663676416 | bytes 4194304 | tf_op jit(solution)/shard_map/pallas_call | solution.py:479
  (177 shorter events, 92.5 us)
Async XLA Ops:
  3.6 18.4 %all-to-all-start = ((s16[8,528,128]{2,1,0:T(8,128)(2,1)}), s16[8,528,128]{2,1,0:T(8,128)(2,1)S(1)}, u32[]{:S(2)}, u32[]{:S(2)}) async-start(s16[8,528,128]{2,1,0:T(8,128)(2,1)} %shard_map.109), calls=%async_computation | async-start | bytes 2162688 | tf_op jit(solution)/shard_map/all_to_all | solution.py:689
  22.0 21.6 %all-to-all-start.1 = ((s16[8,528,128]{2,1,0:T(8,128)(2,1)}), s16[8,528,128]{2,1,0:T(8,128)(2,1)S(1)}, u32[]{:S(2)}, u32[]{:S(2)}) async-start(s16[8,528,128]{2,1,0:T(8,128)(2,1)} %shard_map.110), calls=%async_computation.1 | async-start | bytes 2162688 | tf_op jit(solution)/shard_map/all_to_all | solution.py:689
  43.7 32.8 %all-to-all-start.2 = ((bf16[32,2,64,128]{3,2,1,0:T(8,128)(2,1)}), bf16[32,2,64,128]{3,2,1,0:T(8,128)(2,1)S(1)}, u32[]{:S(2)}, u32[]{:S(2)}) async-start(bf16[32,2,64,128]{3,2,1,0:T(8,128)(2,1)} %get-tuple-element.175), calls=%async_computation.2 | async-start | bytes 2097152 | tf_op jit(solution)/shard_map/all_to_all | solution.py:686
  50.4 20.5 %collective-permute-start = (s16[1056,128]{1,0:T(8,128)(2,1)}, s16[1056,128]{1,0:T(8,128)(2,1)S(1)}, u32[]{:S(2)}, u32[]{:S(2)}) collective-permute-start(s16[1056,128]{1,0:T(8,128)(2,1)} %get-tuple-element.185), channel_id=1, source_target_pairs={{0,2},{1,3},{2,0},{3,1},{4,6},{5,7},{6,4},{7,5},{8,10},{9,11},{10,... | collective-permute-start | bytes 811016 | tf_op jit(solution)/shard_map/ppermute | solution.py:669
  51.9 19.0 %collective-permute-start.1 = (s16[1056,128]{1,0:T(8,128)(2,1)}, s16[1056,128]{1,0:T(8,128)(2,1)S(1)}, u32[]{:S(2)}, u32[]{:S(2)}) collective-permute-start(s16[1056,128]{1,0:T(8,128)(2,1)} %get-tuple-element.186), channel_id=1, source_target_pairs={{0,4},{1,5},{2,6},{3,7},{4,0},{5,1},{6,2},{7,3},{8,12},{9,13},{10,... | collective-permute-start | bytes 811016 | tf_op jit(solution)/shard_map/ppermute | solution.py:669
  53.1 23.4 %collective-permute-start.2 = (s16[1056,128]{1,0:T(8,128)(2,1)S(1)}, s16[1056,128]{1,0:T(8,128)(2,1)S(1)}, u32[]{:S(2)}, u32[]{:S(2)}) collective-permute-start(s16[1056,128]{1,0:T(8,128)(2,1)S(1)} %copy-done.39), channel_id=1, source_target_pairs={{0,6},{1,7},{2,4},{3,5},{4,2},{5,3},{6,0},{7,1},{8,14},{9,15},{10,... | collective-permute-start | bytes 811016 | tf_op jit(solution)/shard_map/ppermute | solution.py:669
  76.5 34.5 %all-to-all-start.3 = ((bf16[32,2,64,128]{3,2,1,0:T(8,128)(2,1)}), bf16[32,2,64,128]{3,2,1,0:T(8,128)(2,1)S(1)}, u32[]{:S(2)}, u32[]{:S(2)}) async-start(bf16[32,2,64,128]{3,2,1,0:T(8,128)(2,1)} %get-tuple-element.193), calls=%async_computation.3 | async-start | bytes 2097152 | tf_op jit(solution)/shard_map/all_to_all | solution.py:686
  85.0 26.0 %collective-permute-start.4 = (s16[1056,128]{1,0:T(8,128)(2,1)}, s16[1056,128]{1,0:T(8,128)(2,1)}, u32[]{:S(2)}, u32[]{:S(2)}) collective-permute-start(s16[1056,128]{1,0:T(8,128)(2,1)} %get-tuple-element.206), channel_id=1, source_target_pairs={{0,2},{1,3},{2,0},{3,1},{4,6},{5,7},{6,4},{7,5},{8,10},{9,11},{10,... | collective-permute-start | bytes 811016 | tf_op jit(solution)/shard_map/ppermute | solution.py:669
  86.5 24.5 %collective-permute-start.5 = (s16[1056,128]{1,0:T(8,128)(2,1)}, s16[1056,128]{1,0:T(8,128)(2,1)}, u32[]{:S(2)}, u32[]{:S(2)}) collective-permute-start(s16[1056,128]{1,0:T(8,128)(2,1)} %get-tuple-element.207), channel_id=1, source_target_pairs={{0,4},{1,5},{2,6},{3,7},{4,0},{5,1},{6,2},{7,3},{8,12},{9,13},{10,... | collective-permute-start | bytes 811016 | tf_op jit(solution)/shard_map/ppermute | solution.py:669
  87.7 23.4 %collective-permute-start.6 = (s16[1056,128]{1,0:T(8,128)(2,1)}, s16[1056,128]{1,0:T(8,128)(2,1)}, u32[]{:S(2)}, u32[]{:S(2)}) collective-permute-start(s16[1056,128]{1,0:T(8,128)(2,1)} %get-tuple-element.208), channel_id=1, source_target_pairs={{0,6},{1,7},{2,4},{3,5},{4,2},{5,3},{6,0},{7,1},{8,14},{9,15},{10,... | collective-permute-start | bytes 811016 | tf_op jit(solution)/shard_map/ppermute | solution.py:669
  113.1 37.2 %all-to-all-start.4 = ((bf16[32,2,64,128]{3,2,1,0:T(8,128)(2,1)}), bf16[32,2,64,128]{3,2,1,0:T(8,128)(2,1)}, u32[]{:S(2)}, u32[]{:S(2)}) async-start(bf16[32,2,64,128]{3,2,1,0:T(8,128)(2,1)} %get-tuple-element.210), calls=%async_computation.4 | async-start | bytes 2097152 | tf_op jit(solution)/shard_map/all_to_all | solution.py:686
  161.1 34.9 %all-to-all-start.5 = ((bf16[32,2,64,128]{3,2,1,0:T(8,128)(2,1)}), bf16[32,2,64,128]{3,2,1,0:T(8,128)(2,1)}, u32[]{:S(2)}, u32[]{:S(2)}) async-start(bf16[32,2,64,128]{3,2,1,0:T(8,128)(2,1)} %copy-done.4), calls=%async_computation.5 | async-start | bytes 2097152 | tf_op jit(solution)/shard_map/all_to_all | solution.py:686
  171.5 23.9 %collective-permute-start.13 = (bf16[2,2,64,128]{3,2,1,0:T(8,128)(2,1)S(1)}, bf16[2,2,64,128]{3,2,1,0:T(8,128)(2,1)S(1)}, u32[]{:S(2)}, u32[]{:S(2)}) collective-permute-start(bf16[2,2,64,128]{3,2,1,0:T(8,128)(2,1)S(1)} %get-tuple-element.241), channel_id=1, source_target_pairs={{0,16},{8,24},{16,0},{24,8},{1,17},{9,25},{17,1},{25,9},{2,18},{10... | collective-permute-start | bytes 196616 | tf_op jit(solution)/shard_map/ppermute | solution.py:669
  173.6 22.4 %collective-permute-start.14 = (bf16[2,2,64,128]{3,2,1,0:T(8,128)(2,1)S(1)}, bf16[2,2,64,128]{3,2,1,0:T(8,128)(2,1)}, u32[]{:S(2)}, u32[]{:S(2)}) collective-permute-start(bf16[2,2,64,128]{3,2,1,0:T(8,128)(2,1)S(1)} %get-tuple-element.242), channel_id=1, source_target_pairs={{0,24},{8,16},{16,8},{24,0},{1,25},{9,17},{17,9},{25,1},{2,26},{10... | collective-permute-start | bytes 196616 | tf_op jit(solution)/shard_map/ppermute | solution.py:669
  196.0 29.6 %all-to-all-start.6 = ((bf16[32,2,64,128]{3,2,1,0:T(8,128)(2,1)}), bf16[32,2,64,128]{3,2,1,0:T(8,128)(2,1)S(1)}, u32[]{:S(2)}, u32[]{:S(2)}) async-start(bf16[32,2,64,128]{3,2,1,0:T(8,128)(2,1)} %copy-done.3), calls=%async_computation.6 | async-start | bytes 2097152 | tf_op jit(solution)/shard_map/all_to_all | solution.py:686
  204.2 20.6 %collective-permute-start.16 = (bf16[8,2,64,128]{3,2,1,0:T(8,128)(2,1)S(1)}, bf16[8,2,64,128]{3,2,1,0:T(8,128)(2,1)S(1)}, u32[]{:S(2)}, u32[]{:S(2)}) collective-permute-start(bf16[8,2,64,128]{3,2,1,0:T(8,128)(2,1)S(1)} %slice_dynamic-update-slice_fusion.refs_0_), channel_id=1, source_target_pairs={{0,4},{1,5},{2,6},{3,7},{4,0},{5,1},{6,2},{7,3},{8,12},{9,13},{10,... | collective-permute-start | bytes 786440 | tf_op jit(solution)/shard_map/ppermute | solution.py:669
  204.5 21.0 %collective-permute-start.15 = (bf16[8,2,64,128]{3,2,1,0:T(8,128)(2,1)S(1)}, bf16[8,2,64,128]{3,2,1,0:T(8,128)(2,1)}, u32[]{:S(2)}, u32[]{:S(2)}) collective-permute-start(bf16[8,2,64,128]{3,2,1,0:T(8,128)(2,1)S(1)} %slice_dynamic-update-slice_fusion.refs_0_), channel_id=1, source_target_pairs={{0,2},{1,3},{2,0},{3,1},{4,6},{5,7},{6,4},{7,5},{8,10},{9,11},{10,... | collective-permute-start | bytes 786440 | tf_op jit(solution)/shard_map/ppermute | solution.py:669
  225.6 32.3 %all-to-all-start.7 = ((bf16[32,2,64,128]{3,2,1,0:T(8,128)(2,1)}), bf16[32,2,64,128]{3,2,1,0:T(8,128)(2,1)S(1)}, u32[]{:S(2)}, u32[]{:S(2)}) async-start(bf16[32,2,64,128]{3,2,1,0:T(8,128)(2,1)} %shard_map.127), calls=%async_computation.7 | async-start | bytes 2097152 | tf_op jit(solution)/shard_map/all_to_all | solution.py:686
  231.8 20.5 %collective-permute-start.18 = (s16[1056,128]{1,0:T(8,128)(2,1)}, s16[1056,128]{1,0:T(8,128)(2,1)S(1)}, u32[]{:S(2)}, u32[]{:S(2)}) collective-permute-start(s16[1056,128]{1,0:T(8,128)(2,1)} %get-tuple-element.259), channel_id=1, source_target_pairs={{0,2},{1,3},{2,0},{3,1},{4,6},{5,7},{6,4},{7,5},{8,10},{9,11},{10,... | collective-permute-start | bytes 811016 | tf_op jit(solution)/shard_map/ppermute | solution.py:669
  233.3 19.1 %collective-permute-start.19 = (s16[1056,128]{1,0:T(8,128)(2,1)}, s16[1056,128]{1,0:T(8,128)(2,1)S(1)}, u32[]{:S(2)}, u32[]{:S(2)}) collective-permute-start(s16[1056,128]{1,0:T(8,128)(2,1)} %get-tuple-element.260), channel_id=1, source_target_pairs={{0,4},{1,5},{2,6},{3,7},{4,0},{5,1},{6,2},{7,3},{8,12},{9,13},{10,... | collective-permute-start | bytes 811016 | tf_op jit(solution)/shard_map/ppermute | solution.py:669
  234.5 23.4 %collective-permute-start.20 = (s16[1056,128]{1,0:T(8,128)(2,1)}, s16[1056,128]{1,0:T(8,128)(2,1)S(1)}, u32[]{:S(2)}, u32[]{:S(2)}) collective-permute-start(s16[1056,128]{1,0:T(8,128)(2,1)} %get-tuple-element.261), channel_id=1, source_target_pairs={{0,6},{1,7},{2,4},{3,5},{4,2},{5,3},{6,0},{7,1},{8,14},{9,15},{10,... | collective-permute-start | bytes 811016 | tf_op jit(solution)/shard_map/ppermute | solution.py:669
  236.5 21.4 %collective-permute-start.21 = (bf16[16,2,64,128]{3,2,1,0:T(8,128)(2,1)}, bf16[16,2,64,128]{3,2,1,0:T(8,128)(2,1)S(1)}, u32[]{:S(2)}, u32[]{:S(2)}) collective-permute-start(bf16[16,2,64,128]{3,2,1,0:T(8,128)(2,1)} %shard_map.131), channel_id=1, source_target_pairs={{0,1},{1,0},{2,3},{3,2},{4,5},{5,4},{6,7},{7,6},{8,9},{9,8},{10,11... | collective-permute-start | bytes 1572872 | tf_op jit(solution)/shard_map/ppermute | solution.py:669
  258.9 21.8 %all-to-all-start.8 = ((s16[8,528,128]{2,1,0:T(8,128)(2,1)}), s16[8,528,128]{2,1,0:T(8,128)(2,1)S(1)}, u32[]{:S(2)}, u32[]{:S(2)}) async-start(s16[8,528,128]{2,1,0:T(8,128)(2,1)} %bitcast.37), calls=%async_computation.8 | async-start | bytes 2162688 | tf_op jit(solution)/shard_map/all_to_all | solution.py:689
  280.8 24.8 %all-to-all-start.9 = ((s16[8,528,128]{2,1,0:T(8,128)(2,1)}), s16[8,528,128]{2,1,0:T(8,128)(2,1)S(1)}, u32[]{:S(2)}, u32[]{:S(2)}) async-start(s16[8,528,128]{2,1,0:T(8,128)(2,1)} %bitcast.38), calls=%async_computation.9 | async-start | bytes 2162688 | tf_op jit(solution)/shard_map/all_to_all | solution.py:689
  (50 other events, 383.9 us)
where the time goes:
time: 317 us; the launch traced here: 312 us
  Pallas kernels  186 us (59%)
  starting transfers between devices  74.9 us (24%)
  waiting for transfers between devices  32.8 us (10%)
  local copies, waits for them, and re-layouts  12.1 us (4%)
  between operations  5.38 us (2%)
    pallas_call x4, Pallas kernels, first_round(): pl.pallas_call(functools.partial(first_kernel, plan, shared, pieces), in_...  60.7 us
    pallas_call x4, Pallas kernels, second_round(): pl.pallas_call(functools.partial(second_kernel, plan, shared, natural, pi...  58.8 us
    all_to_all x6, starting transfers between devices, over_all(): return lax.all_to_all(piece, ('chan', 'rad'), 0, 0, tiled=True)  33 us
    ppermute x24, waiting for transfers between devices, over(): return lax.ppermute(piece, axis, [(i, i ^ d) for i in range(size)])  32.7 us
    ppermute x24, starting transfers between devices, over(): return lax.ppermute(piece, axis, [(i, i ^ d) for i in range(size)])  21 us
    all_to_all x4, starting transfers between devices, share(): lax.all_to_all(piece.reshape(rad, -1, LANES), 'rad', 0, 0, tiled=True)  20.9 us
    pallas_call x4, Pallas kernels, couple_round(): pl.pallas_call(functools.partial(couple_kernel, len(gathered), at, per, s...  19 us
    pallas_call x4, Pallas kernels, encode_rounds(): pl.pallas_call(functools.partial(encode_kernel, rounds, natural), grid=(1...  11.6 us
  transfers between devices with their start and end apart: 34, of which 7 were waited for; matrix products, arithmetic and copies ran while one was open for 1% of the time, Pallas kernels for 54%

commit v1 on v0

--- a/solution.py
+++ b/solution.py
@@ -181,38 +181,45 @@
         return at if self.natural else me ^ at
 
 
-def decode_kernel(live, rows, points, pieces, spot_ref, *refs):
+def decode_kernel(lives, rows, points, given, spot_ref, *refs):
     out_ref = refs[-1]
-    for d, piece in enumerate(refs[:-2]):
-        slot = slot_to(pieces.place(d, spot_ref[0]), live)
-
-        def write():
-            def put(q, row, column, value):
-                out_ref[0, q, slot, pl.ds(row, GROUP_ROWS), pl.ds(column, LANES)] = value
-
-            decode_piece(lambda row: piece[pl.ds(row, GROUP_ROWS), :], rows, points, put)
-
-        if live & (live - 1) == 0:
-            write()
-        elif d < live:
-            write()
-
-
-def decode_round(pieces, total, start, live, spot, shape):
+    first, base = 0, 0
+    for live, pieces in zip(lives, given):
+        for d in range(len(pieces.blocks)):
+            piece = refs[first + d]
+            slot = base + slot_to(pieces.place(d, spot_ref[0]), live)
+
+            def write():
+                def put(q, row, column, value):
+                    out_ref[0, q, slot, pl.ds(row, GROUP_ROWS), pl.ds(column, LANES)] = value
+
+                decode_piece(lambda row: piece[pl.ds(row, GROUP_ROWS), :], rows, points, put)
+
+            if live & (live - 1) == 0:
+                write()
+            elif d < live:
+                write()
+        first, base = first + len(pieces.blocks), base + live
+
+
+def decode_rounds(given, total, rounds, spot, shape):
     _, _, _, rows, points = shape
     size = piece_rows(rows, points)
-    count = len(pieces.blocks)
-    aliases = {} if total is None else {1 + count: 0}
+    arrays = [array for pieces in given for array in pieces.arrays()]
+    specs = [spec for pieces in given for spec in pieces.specs(size)]
+    start, lives = rounds[0][0], [live for _, live in rounds]
+    count = sum(lives)
+    aliases = {} if total is None else {1 + len(arrays): 0}
     return pl.pallas_call(
-        functools.partial(decode_kernel, live, rows, points, pieces),
+        functools.partial(decode_kernel, lives, rows, points, given),
         grid=(1,),
-        in_specs=[SMEM] + pieces.specs(size) + [ANY],
-        out_specs=pl.BlockSpec((1, 2, live, rows, points), lambda i: (0, 0, start // live, 0, 0)),
+        in_specs=[SMEM] + specs + [ANY],
+        out_specs=pl.BlockSpec((1, 2, count, rows, points), lambda i: (0, 0, start // count, 0, 0)),
         out_shape=jax.ShapeDtypeStruct(shape, f32),
         input_output_aliases=aliases,
         compiler_params=ROOM,
-        cost_estimate=pl.CostEstimate(flops=0, bytes_accessed=6 * live * size * LANES, transcendentals=0),
-    )(spot, *pieces.arrays(), spot if total is None else total)
+        cost_estimate=pl.CostEstimate(flops=0, bytes_accessed=6 * count * size * LANES, transcendentals=0),
+    )(spot, *arrays, spot if total is None else total)
 
 
 def split(value):
@@ -671,9 +678,8 @@
     def over_even(arrays):
         return [arrays[0]] + [over(array, "rad", rad, 2 * e) for e, array in enumerate(arrays) if e]
 
-    def over_next(got, count):
-        half = got[0].shape[0] // 2
-        swapped = over(second_halves(got), "rad", rad, 1)
+    def over_next(got, count, halves=None):
+        swapped = over(second_halves(got) if halves is None else halves, "rad", rad, 1)
         return [
             Pieces([(swapped, (d // 2) * count + j) if d % 2 else (got[d // 2], j) for d in range(rad)], False)
             for j in range(count)
@@ -726,7 +732,7 @@
         col_ids = (z % column_cuts) * LANES + jnp.arange(LANES, dtype=i32)
         return weights, kernel_table(row_ids, col_ids, points).reshape(4, height // PACK, PACK * LANES)
 
-    firsts, gathered, arriving, fixed = [], [], (), None
+    firsts, gathered, arriving, fixed, halves = [], [], (), None, None
     first, pieces = apply_first(received)
     firsts.append(first)
     if len(near) > 1:
@@ -735,19 +741,20 @@
     for j in range(1, len(rounds)):
         flying = over_all(flying)
         if j > 1:
-            received = over_next(arriving, 1)[0]
+            received = over_next(arriving, 1, halves)[0]
         arriving = over_even(far[j - 1]) if j - 1 < len(far) else ()
         if j == 1:
             far += [encode_rounds(later, [r], rad, spot, False) for r in rounds[3:]]
-        if j == 2:
+        if j == full:
             fixed = constants(small)
         first, pieces = apply_first(received, live if j == full else None)
         firsts.append(first)
         if j == full:
             pieces = [pieces[0]] + [over(piece, "rad", rad, d) for d, piece in enumerate(pieces) if d]
             pieces = over_chan([jnp.stack([piece[e] for piece in pieces]) for e in range(chan)])
-        flown, pieces, small, far, arriving, gathered, fixed = cut(
-            (flying, pieces, small, far, arriving, gathered, fixed)
+        halves = second_halves(arriving) if arriving and j > 1 else None
+        flown, pieces, small, far, arriving, gathered, fixed, halves = cut(
+            (flying, pieces, small, far, arriving, gathered, fixed, halves)
         )
         flying = pieces[0]
         gathered.append(gather_round([flown], spot, everyone))
@@ -792,16 +799,16 @@
     update = apply_second(mine, full - 1)
     update, ready, shared = cut((update, ready, shared))
     done = share(update[0])
-    for j, pieces in enumerate(ready):
-        total = decode_round(pieces, total, *rounds[j], spot, vectors.shape)
+    if ready:
+        total = decode_rounds(ready, total, rounds[: len(ready)], spot, vectors.shape)
     if live:
         extra = apply_second(shared, full, live)
         done, extra, total = cut((done, extra, total))
         extra = [extra[0]] + [over(piece, "rad", rad, d) for d, piece in enumerate(extra) if d]
         extra = Pieces([(piece, 0) for piece in extra], False)
-    total = decode_round(done, total, *rounds[full - 1], spot, vectors.shape)
+    total = decode_rounds([done], total, rounds[full - 1 : full], spot, vectors.shape)
     if live:
-        total = decode_round(extra, total, *rounds[full], spot, vectors.shape)
+        total = decode_rounds([extra], total, rounds[full:], spot, vectors.shape)
     return total
 
 

time: 317 us -> 331 us (1.044)
  waiting for transfers between devices: 32.8 us -> 52.2 us
  starting transfers between devices: 74.9 us -> 70.7 us
    ppermute x24, waiting for transfers between devices: 32.7 us -> 52.1 us  [over(): return lax.ppermute(piece, axis, [(i, i ^ d) for i in range(size)])]
    pallas_call x4 -> x3, Pallas kernels: 10.4 us -> 8.78 us  [decode_rounds(): pl.pallas_call(functools.partial(decode_kernel, lives, rows, points, give...]
    unnamed x87 -> x95, local copies, waits for them, and re-layouts: 9.81 us -> 10.3 us
  transfers between devices with their start and end apart: 34 -> 34, of which waited for: 7 -> 9; matrix products, arithmetic and copies ran while one was open for 1% -> 1% of each run, Pallas kernels for 54% -> 52%
where the time goes in v1:
time: 331 us; the launch traced here: 326 us
  Pallas kernels  184 us (56%)
  starting transfers between devices  70.7 us (21%)
  waiting for transfers between devices  52.2 us (16%)
  local copies, waits for them, and re-layouts  12.6 us (4%)
  between operations  5.73 us (2%)
    pallas_call x4, Pallas kernels, first_round(): pl.pallas_call(functools.partial(first_kernel, plan, shared, pieces), in_...  60.7 us
    pallas_call x4, Pallas kernels, second_round(): pl.pallas_call(functools.partial(second_kernel, plan, shared, natural, pi...  58.8 us
    ppermute x24, waiting for transfers between devices, over(): return lax.ppermute(piece, axis, [(i, i ^ d) for i in range(size)])  52.1 us
    all_to_all x6, starting transfers between devices, over_all(): return lax.all_to_all(piece, ('chan', 'rad'), 0, 0, tiled=True)  29.9 us
    all_to_all x4, starting transfers between devices, share(): lax.all_to_all(piece.reshape(rad, -1, LANES), 'rad', 0, 0, tiled=True)  20.8 us
    ppermute x24, starting transfers between devices, over(): return lax.ppermute(piece, axis, [(i, i ^ d) for i in range(size)])  20 us
    pallas_call x4, Pallas kernels, couple_round(): pl.pallas_call(functools.partial(couple_kernel, len(gathered), at, per, s...  19 us
    pallas_call x4, Pallas kernels, encode_rounds(): pl.pallas_call(functools.partial(encode_kernel, rounds, natural), grid=(1...  11.5 us
  transfers between devices with their start and end apart: 34, of which 9 were waited for; matrix products, arithmetic and copies ran while one was open for 1% of the time, Pallas kernels for 52%

profile of v1, /device:TPU:1, one launch (start us, length us, event | category | flops | bytes accessed | tf_op | source)
XLA Modules:
  0.0 326.5 jit_solution(11652891469754033545)
XLA Ops:
  3.6 5.2 %all-to-all-start = ((s16[8,528,128]{2,1,0:T(8,128)(2,1)}), s16[8,528,128]{2,1,0:T(8,128)(2,1)S(1)}, u32[]{:S(2)}, u32[]{:S(2)}) async-start(s16[8,528,128]{2,1,0:T(8,128)(2,1)} %shard_map.109), calls=%async_computation | async-start | bytes 2162688 | tf_op jit(solution)/shard_map/all_to_all | solution.py:695
  16.2 5.8 %shard_map.112 = (bf16[6,512,512]{2,1,0:T(8,128)(2,1)}, bf16[6,512,512]{2,1,0:T(8,128)(2,1)}, f32[2,512,512]{2,1,0:T(8,128)}) custom-call(f32[1]{0:T(128)S(6)} %copy.23.shift_energy_ref, f32[1]{0:T(128)S(6)} %copy.24.shift_width_ref, f32[2,512,512]{2,1,0:T(8,128)} %vec_ref.1, f32[1,512]{1,0:T(1,128)} %bitcast.58, f32[1,512]{1,0:T(1,128)} %bitcast.59), custom_call_target="tpu_custom_call" | custom-call | bytes 6291456 | tf_op jit(solution)/shard_map/pallas_call | solution.py:327
  22.0 6.4 %all-to-all-start.1 = ((s16[8,528,128]{2,1,0:T(8,128)(2,1)}), s16[8,528,128]{2,1,0:T(8,128)(2,1)S(1)}, u32[]{:S(2)}, u32[]{:S(2)}) async-start(s16[8,528,128]{2,1,0:T(8,128)(2,1)} %shard_map.110), calls=%async_computation.1 | async-start | bytes 2162688 | tf_op jit(solution)/shard_map/all_to_all | solution.py:695
  28.4 15.2 %shard_map.113 = (f32[2,512,512]{2,1,0:T(8,128)}, bf16[32,2,64,128]{3,2,1,0:T(8,128)(2,1)}) custom-call(s32[2]{0:T(128)} %pad_add_fusion.spot_ref.refs_16_, s16[4224,128]{1,0:T(8,128)(2,1)} %bitcast.39, s16[4224,128]{1,0:T(8,128)(2,1)} %bitcast.40, s16[4224,128]{1,0:T(8,128)(2,1)} %bitcast.41, s16[4224,128]{1,0:T(8,128)(2,1)} %bitcast.42, ...), custom_call_target="tpu_custom_call" | custom-call | flops 9663676416 | bytes 4194304 | tf_op jit(solution)/shard_map/pallas_call | solution.py:397
  43.7 6.7 %all-to-all-start.2 = ((bf16[32,2,64,128]{3,2,1,0:T(8,128)(2,1)}), bf16[32,2,64,128]{3,2,1,0:T(8,128)(2,1)S(1)}, u32[]{:S(2)}, u32[]{:S(2)}) async-start(bf16[32,2,64,128]{3,2,1,0:T(8,128)(2,1)} %get-tuple-element.180), calls=%async_computation.2 | async-start | bytes 2097152 | tf_op jit(solution)/shard_map/all_to_all | solution.py:692
  53.1 15.2 %shard_map.114 = (f32[2,512,512]{2,1,0:T(8,128)}, bf16[32,2,64,128]{3,2,1,0:T(8,128)(2,1)}) custom-call(s32[2]{0:T(128)} %pad_add_fusion.spot_ref.refs_16_, s16[4224,128]{1,0:T(8,128)(2,1)} %bitcast.47, s16[4224,128]{1,0:T(8,128)(2,1)} %bitcast.48, s16[4224,128]{1,0:T(8,128)(2,1)} %bitcast.49, s16[4224,128]{1,0:T(8,128)(2,1)} %bitcast.50, ...), custom_call_target="tpu_custom_call" | custom-call | flops 9663676416 | bytes 4194304 | tf_op jit(solution)/shard_map/pallas_call | solution.py:397
  70.9 5.6 %collective-permute-done.2.refs_3_.refs_6_ = s16[1056,128]{1,0:T(8,128)(2,1)S(1)} collective-permute-done((s16[1056,128]{1,0:T(8,128)(2,1)S(1)}, s16[1056,128]{1,0:T(8,128)(2,1)S(1)}, u32[]{:S(2)}, u32[]{:S(2)}) %collective-permute-start.2) | collective-permute-done | bytes 270368 | tf_op jit(solution)/shard_map/ppermute | solution.py:676
  76.5 4.7 %all-to-all-start.3 = ((bf16[32,2,64,128]{3,2,1,0:T(8,128)(2,1)}), bf16[32,2,64,128]{3,2,1,0:T(8,128)(2,1)S(1)}, u32[]{:S(2)}, u32[]{:S(2)}) async-start(bf16[32,2,64,128]{3,2,1,0:T(8,128)(2,1)} %get-tuple-element.198), calls=%async_computation.3 | async-start | bytes 2097152 | tf_op jit(solution)/shard_map/all_to_all | solution.py:692
  88.1 11.0 %collective-permute-done.4.refs_1_.refs_2_ = s16[1056,128]{1,0:T(8,128)(2,1)S(1)} collective-permute-done((s16[1056,128]{1,0:T(8,128)(2,1)}, s16[1056,128]{1,0:T(8,128)(2,1)S(1)}, u32[]{:S(2)}, u32[]{:S(2)}) %collective-permute-start.4) | collective-permute-done | bytes 270368 | tf_op jit(solution)/shard_map/ppermute | solution.py:676
  99.1 8.4 %collective-permute-done.6.refs_3_.refs_6_ = s16[1056,128]{1,0:T(8,128)(2,1)S(1)} collective-permute-done((s16[1056,128]{1,0:T(8,128)(2,1)}, s16[1056,128]{1,0:T(8,128)(2,1)S(1)}, u32[]{:S(2)}, u32[]{:S(2)}) %collective-permute-start.6) | collective-permute-done | bytes 270368 | tf_op jit(solution)/shard_map/ppermute | solution.py:676
  110.2 15.3 %shard_map.117 = (f32[2,512,512]{2,1,0:T(8,128)}, bf16[32,2,64,128]{3,2,1,0:T(8,128)(2,1)}) custom-call(s32[2]{0:T(128)} %pad_add_fusion.spot_ref.refs_16_, s16[1056,128]{1,0:T(8,128)(2,1)} %get-tuple-element.199.refs_0_, s16[2112,128]{1,0:T(8,128)(2,1)} %collective-permute-done.3.refs_1_.refs_3_.refs_5_.refs_7_, s16[1056,128]{1,0:T(8,128)(2,1)} %copy-done.31, ...), custom_call_target="tpu_custom_call" | custom-call | flops 9663676416 | bytes 4194304 | tf_op jit(solution)/shard_map/pallas_call | solution.py:397
  139.5 15.0 %shard_map.120 = (f32[2,512,512]{2,1,0:T(8,128)}, bf16[4,2,64,128]{3,2,1,0:T(8,128)(2,1)}, bf16[4,2,64,128]{3,2,1,0:T(8,128)(2,1)}) custom-call(s32[2]{0:T(128)} %pad_add_fusion.spot_ref.refs_16_, s16[1056,128]{1,0:T(8,128)(2,1)} %get-tuple-element.216.refs_0_, s16[2112,128]{1,0:T(8,128)(2,1)} %collective-permute-done.7.refs_1_.refs_3_.refs_5_.refs_7_, ...), custom_call_target="tpu_custom_call" | custom-call | flops 9663676416 | bytes 4194304 | tf_op jit(solution)/shard_map/pallas_call | solution.py:397
  171.4 4.9 %shard_map.125 = bf16[32,2,64,128]{3,2,1,0:T(8,128)(2,1)S(1)} custom-call(s32[2]{0:T(128)S(1)} %copy-done.8, bf16[4,128,256]{2,1,0:T(8,128)(2,1)S(1)} %copy-done.2, f32[4,16,512]{2,1,0:T(8,128)S(1)} %pad_maximum_fusion.table_ref, bf16[2,16,32,512]{3,2,1,0:T(8,128)(2,1)S(1)} %shard_map.118.refs_0_, bf16[2,16,32,512]{3,2,1,0:T(8,128)(2,1)S(1)} %shard_map.121.refs_1_, ...), custom_call_target="tpu_custom_call" | custom-call | flops 2147483648 | bytes 6291456 | tf_op jit(solution)/shard_map/pallas_call | solution.py:629
  177.4 5.3 %all-to-all-start.5 = ((bf16[32,2,64,128]{3,2,1,0:T(8,128)(2,1)}), bf16[32,2,64,128]{3,2,1,0:T(8,128)(2,1)}, u32[]{:S(2)}, u32[]{:S(2)}) async-start(bf16[32,2,64,128]{3,2,1,0:T(8,128)(2,1)} %copy-done.4), calls=%async_computation.5 | async-start | bytes 2097152 | tf_op jit(solution)/shard_map/all_to_all | solution.py:692
  191.2 5.9 %shard_map.127 = bf16[32,2,64,128]{3,2,1,0:T(8,128)(2,1)} custom-call(s32[2]{0:T(128)S(1)} %copy-done.8, bf16[4,128,256]{2,1,0:T(8,128)(2,1)S(1)} %copy-done.2, f32[4,16,512]{2,1,0:T(8,128)S(1)} %pad_maximum_fusion.table_ref, bf16[2,16,32,512]{3,2,1,0:T(8,128)(2,1)S(1)} %shard_map.118.refs_0_, bf16[2,16,32,512]{3,2,1,0:T(8,128)(2,1)S(1)} %shard_map.121.refs_1_, ...), custom_call_target="tpu_custom_call" | custom-call | flops 2147483648 | bytes 6291456 | tf_op jit(solution)/shard_map/pallas_call | solution.py:629
  197.1 4.9 %shard_map.126 = bf16[32,2,64,128]{3,2,1,0:T(8,128)(2,1)S(1)} custom-call(s32[2]{0:T(128)S(1)} %copy-done.8, bf16[4,128,256]{2,1,0:T(8,128)(2,1)S(1)} %copy-done.2, f32[4,16,512]{2,1,0:T(8,128)S(1)} %pad_maximum_fusion.table_ref, bf16[2,16,32,512]{3,2,1,0:T(8,128)(2,1)S(1)} %shard_map.118.refs_0_, bf16[2,16,32,512]{3,2,1,0:T(8,128)(2,1)S(1)} %shard_map.121.refs_1_, ...), custom_call_target="tpu_custom_call" | custom-call | flops 2147483648 | bytes 6291456 | tf_op jit(solution)/shard_map/pallas_call | solution.py:629
  203.0 9.4 %collective-permute-done.13 = bf16[2,2,64,128]{3,2,1,0:T(8,128)(2,1)S(1)} collective-permute-done((bf16[2,2,64,128]{3,2,1,0:T(8,128)(2,1)S(1)}, bf16[2,2,64,128]{3,2,1,0:T(8,128)(2,1)S(1)}, u32[]{:S(2)}, u32[]{:S(2)}) %collective-permute-start.13) | collective-permute-done | bytes 65568 | tf_op jit(solution)/shard_map/ppermute | solution.py:676
  222.4 14.7 %shard_map.129 = (s16[1056,128]{1,0:T(8,128)(2,1)}, s16[1056,128]{1,0:T(8,128)(2,1)}, s16[1056,128]{1,0:T(8,128)(2,1)}, s16[1056,128]{1,0:T(8,128)(2,1)}) custom-call(s32[2]{0:T(128)} %pad_add_fusion.spot_ref.refs_16_, bf16[32,2,64,128]{3,2,1,0:T(8,128)(2,1)} %all-to-all-done.5.refs_0_, bf16[6,512,512]{2,1,0:T(8,128)(2,1)} %get-tuple-element.164.refs_8_.refs_1_, ...), custom_call_target="tpu_custom_call" | custom-call | flops 9663676416 | bytes 4194304 | tf_op jit(solution)/shard_map/pallas_call | solution.py:486
  237.2 6.7 %collective-permute-done.17.refs_3_.refs_6_ = bf16[8,2,64,128]{3,2,1,0:T(8,128)(2,1)S(1)} collective-permute-done((bf16[8,2,64,128]{3,2,1,0:T(8,128)(2,1)S(1)}, bf16[8,2,64,128]{3,2,1,0:T(8,128)(2,1)S(1)}, u32[]{:S(2)}, u32[]{:S(2)}) %collective-permute-start.17) | collective-permute-done | bytes 262176 | tf_op jit(solution)/shard_map/ppermute | solution.py:676
  243.9 4.9 %all-to-all-start.7 = ((bf16[32,2,64,128]{3,2,1,0:T(8,128)(2,1)}), bf16[32,2,64,128]{3,2,1,0:T(8,128)(2,1)S(1)}, u32[]{:S(2)}, u32[]{:S(2)}) async-start(bf16[32,2,64,128]{3,2,1,0:T(8,128)(2,1)} %shard_map.127), calls=%async_computation.7 | async-start | bytes 2097152 | tf_op jit(solution)/shard_map/all_to_all | solution.py:692
  253.8 14.8 %shard_map.130 = s16[4224,128]{1,0:T(8,128)(2,1)} custom-call(s32[2]{0:T(128)} %pad_add_fusion.spot_ref.refs_16_, bf16[32,2,64,128]{3,2,1,0:T(8,128)(2,1)} %copy-done.25, bf16[6,512,512]{2,1,0:T(8,128)(2,1)} %get-tuple-element.164.refs_8_.refs_1_, bf16[6,512,512]{2,1,0:T(8,128)(2,1)} %get-tuple-element.165.refs_9_.refs_2_, ...), custom_call_target="tpu_custom_call" | custom-call | flops 9663676416 | bytes 4194304 | tf_op jit(solution)/shard_map/pallas_call | solution.py:486
  268.6 6.5 %collective-permute-done.20.refs_3_.refs_6_ = s16[1056,128]{1,0:T(8,128)(2,1)S(1)} collective-permute-done((s16[1056,128]{1,0:T(8,128)(2,1)S(1)}, s16[1056,128]{1,0:T(8,128)(2,1)S(1)}, u32[]{:S(2)}, u32[]{:S(2)}) %collective-permute-start.20) | collective-permute-done | bytes 270368 | tf_op jit(solution)/shard_map/ppermute | solution.py:676
  281.8 14.8 %shard_map.132 = s16[4224,128]{1,0:T(8,128)(2,1)} custom-call(s32[2]{0:T(128)} %pad_add_fusion.spot_ref.refs_16_, bf16[32,2,64,128]{3,2,1,0:T(8,128)(2,1)} %copy-done.26, bf16[6,512,512]{2,1,0:T(8,128)(2,1)} %get-tuple-element.164.refs_8_.refs_1_, bf16[6,512,512]{2,1,0:T(8,128)(2,1)} %get-tuple-element.165.refs_9_.refs_2_, ...), custom_call_target="tpu_custom_call" | custom-call | flops 9663676416 | bytes 4194304 | tf_op jit(solution)/shard_map/pallas_call | solution.py:486
  305.3 14.6 %shard_map.134 = (s16[528,128]{1,0:T(8,128)(2,1)}, s16[528,128]{1,0:T(8,128)(2,1)}) custom-call(s32[2]{0:T(128)} %pad_add_fusion.spot_ref.refs_16_, bf16[8,2,64,128]{3,2,1,0:T(8,128)(2,1)} %copy-done.27, bf16[16,2,64,128]{3,2,1,0:T(8,128)(2,1)} %collective-permute-done.21.refs_1_.refs_3_.refs_5_.refs_7_, bf16[8,2,64,128]{3,2,1,0:T(8,128)(2,1)} %copy-done.34, ...), custom_call_target="tpu_custom_call" | custom-call | flops 9663676416 | bytes 4194304 | tf_op jit(solution)/shard_map/pallas_call | solution.py:486
  (184 shorter events, 98.8 us)
Async XLA Ops:
  3.6 18.4 %all-to-all-start = ((s16[8,528,128]{2,1,0:T(8,128)(2,1)}), s16[8,528,128]{2,1,0:T(8,128)(2,1)S(1)}, u32[]{:S(2)}, u32[]{:S(2)}) async-start(s16[8,528,128]{2,1,0:T(8,128)(2,1)} %shard_map.109), calls=%async_computation | async-start | bytes 2162688 | tf_op jit(solution)/shard_map/all_to_all | solution.py:695
  22.0 21.6 %all-to-all-start.1 = ((s16[8,528,128]{2,1,0:T(8,128)(2,1)}), s16[8,528,128]{2,1,0:T(8,128)(2,1)S(1)}, u32[]{:S(2)}, u32[]{:S(2)}) async-start(s16[8,528,128]{2,1,0:T(8,128)(2,1)} %shard_map.110), calls=%async_computation.1 | async-start | bytes 2162688 | tf_op jit(solution)/shard_map/all_to_all | solution.py:695
  43.7 32.8 %all-to-all-start.2 = ((bf16[32,2,64,128]{3,2,1,0:T(8,128)(2,1)}), bf16[32,2,64,128]{3,2,1,0:T(8,128)(2,1)S(1)}, u32[]{:S(2)}, u32[]{:S(2)}) async-start(bf16[32,2,64,128]{3,2,1,0:T(8,128)(2,1)} %get-tuple-element.180), calls=%async_computation.2 | async-start | bytes 2097152 | tf_op jit(solution)/shard_map/all_to_all | solution.py:692
  50.4 20.5 %collective-permute-start = (s16[1056,128]{1,0:T(8,128)(2,1)}, s16[1056,128]{1,0:T(8,128)(2,1)S(1)}, u32[]{:S(2)}, u32[]{:S(2)}) collective-permute-start(s16[1056,128]{1,0:T(8,128)(2,1)} %get-tuple-element.190), channel_id=1, source_target_pairs={{0,2},{1,3},{2,0},{3,1},{4,6},{5,7},{6,4},{7,5},{8,10},{9,11},{10,... | collective-permute-start | bytes 811016 | tf_op jit(solution)/shard_map/ppermute | solution.py:676
  51.9 19.0 %collective-permute-start.1 = (s16[1056,128]{1,0:T(8,128)(2,1)}, s16[1056,128]{1,0:T(8,128)(2,1)S(1)}, u32[]{:S(2)}, u32[]{:S(2)}) collective-permute-start(s16[1056,128]{1,0:T(8,128)(2,1)} %get-tuple-element.191), channel_id=1, source_target_pairs={{0,4},{1,5},{2,6},{3,7},{4,0},{5,1},{6,2},{7,3},{8,12},{9,13},{10,... | collective-permute-start | bytes 811016 | tf_op jit(solution)/shard_map/ppermute | solution.py:676
  53.1 23.4 %collective-permute-start.2 = (s16[1056,128]{1,0:T(8,128)(2,1)S(1)}, s16[1056,128]{1,0:T(8,128)(2,1)S(1)}, u32[]{:S(2)}, u32[]{:S(2)}) collective-permute-start(s16[1056,128]{1,0:T(8,128)(2,1)S(1)} %copy-done.42), channel_id=1, source_target_pairs={{0,6},{1,7},{2,4},{3,5},{4,2},{5,3},{6,0},{7,1},{8,14},{9,15},{10,... | collective-permute-start | bytes 811016 | tf_op jit(solution)/shard_map/ppermute | solution.py:676
  76.5 48.9 %all-to-all-start.3 = ((bf16[32,2,64,128]{3,2,1,0:T(8,128)(2,1)}), bf16[32,2,64,128]{3,2,1,0:T(8,128)(2,1)S(1)}, u32[]{:S(2)}, u32[]{:S(2)}) async-start(bf16[32,2,64,128]{3,2,1,0:T(8,128)(2,1)} %get-tuple-element.198), calls=%async_computation.3 | async-start | bytes 2097152 | tf_op jit(solution)/shard_map/all_to_all | solution.py:692
  83.2 27.0 %collective-permute-start.3 = (s16[2112,128]{1,0:T(8,128)(2,1)}, s16[2112,128]{1,0:T(8,128)(2,1)}, u32[]{:S(2)}, u32[]{:S(2)}) collective-permute-start(s16[2112,128]{1,0:T(8,128)(2,1)} %shard_map.116), channel_id=1, source_target_pairs={{0,1},{1,0},{2,3},{3,2},{4,5},{5,4},{6,7},{7,6},{8,9},{9,8},{10,11... | collective-permute-start | bytes 1622024 | tf_op jit(solution)/shard_map/ppermute | solution.py:676
  86.2 21.3 %collective-permute-start.6 = (s16[1056,128]{1,0:T(8,128)(2,1)}, s16[1056,128]{1,0:T(8,128)(2,1)S(1)}, u32[]{:S(2)}, u32[]{:S(2)}) collective-permute-start(s16[1056,128]{1,0:T(8,128)(2,1)} %get-tuple-element.213), channel_id=1, source_target_pairs={{0,6},{1,7},{2,4},{3,5},{4,2},{5,3},{6,0},{7,1},{8,14},{9,15},{10,... | collective-permute-start | bytes 811016 | tf_op jit(solution)/shard_map/ppermute | solution.py:676
  130.5 36.1 %all-to-all-start.4 = ((bf16[32,2,64,128]{3,2,1,0:T(8,128)(2,1)}), bf16[32,2,64,128]{3,2,1,0:T(8,128)(2,1)}, u32[]{:S(2)}, u32[]{:S(2)}) async-start(bf16[32,2,64,128]{3,2,1,0:T(8,128)(2,1)} %get-tuple-element.215), calls=%async_computation.4 | async-start | bytes 2097152 | tf_op jit(solution)/shard_map/all_to_all | solution.py:692
  177.4 35.7 %all-to-all-start.5 = ((bf16[32,2,64,128]{3,2,1,0:T(8,128)(2,1)}), bf16[32,2,64,128]{3,2,1,0:T(8,128)(2,1)}, u32[]{:S(2)}, u32[]{:S(2)}) async-start(bf16[32,2,64,128]{3,2,1,0:T(8,128)(2,1)} %copy-done.4), calls=%async_computation.5 | async-start | bytes 2097152 | tf_op jit(solution)/shard_map/all_to_all | solution.py:692
  189.1 23.4 %collective-permute-start.13 = (bf16[2,2,64,128]{3,2,1,0:T(8,128)(2,1)S(1)}, bf16[2,2,64,128]{3,2,1,0:T(8,128)(2,1)S(1)}, u32[]{:S(2)}, u32[]{:S(2)}) collective-permute-start(bf16[2,2,64,128]{3,2,1,0:T(8,128)(2,1)S(1)} %get-tuple-element.251), channel_id=1, source_target_pairs={{0,16},{8,24},{16,0},{24,8},{1,17},{9,25},{17,1},{25,9},{2,18},{10... | collective-permute-start | bytes 196616 | tf_op jit(solution)/shard_map/ppermute | solution.py:676
  191.2 21.9 %collective-permute-start.14 = (bf16[2,2,64,128]{3,2,1,0:T(8,128)(2,1)S(1)}, bf16[2,2,64,128]{3,2,1,0:T(8,128)(2,1)}, u32[]{:S(2)}, u32[]{:S(2)}) collective-permute-start(bf16[2,2,64,128]{3,2,1,0:T(8,128)(2,1)S(1)} %get-tuple-element.252), channel_id=1, source_target_pairs={{0,24},{8,16},{16,8},{24,0},{1,25},{9,17},{17,9},{25,1},{2,26},{10... | collective-permute-start | bytes 196616 | tf_op jit(solution)/shard_map/ppermute | solution.py:676
  213.8 30.1 %all-to-all-start.6 = ((bf16[32,2,64,128]{3,2,1,0:T(8,128)(2,1)}), bf16[32,2,64,128]{3,2,1,0:T(8,128)(2,1)S(1)}, u32[]{:S(2)}, u32[]{:S(2)}) async-start(bf16[32,2,64,128]{3,2,1,0:T(8,128)(2,1)} %copy-done.3), calls=%async_computation.6 | async-start | bytes 2097152 | tf_op jit(solution)/shard_map/all_to_all | solution.py:692
  219.8 17.4 %collective-permute-start.15 = (bf16[8,2,64,128]{3,2,1,0:T(8,128)(2,1)S(1)}, bf16[8,2,64,128]{3,2,1,0:T(8,128)(2,1)S(1)}, u32[]{:S(2)}, u32[]{:S(2)}) collective-permute-start(bf16[8,2,64,128]{3,2,1,0:T(8,128)(2,1)S(1)} %slice_dynamic-update-slice_fusion.refs_0_), channel_id=1, source_target_pairs={{0,2},{1,3},{2,0},{3,1},{4,6},{5,7},{6,4},{7,5},{8,10},{9,11},{10,... | collective-permute-start | bytes 786440 | tf_op jit(solution)/shard_map/ppermute | solution.py:676
  221.2 16.0 %collective-permute-start.16 = (bf16[8,2,64,128]{3,2,1,0:T(8,128)(2,1)S(1)}, bf16[8,2,64,128]{3,2,1,0:T(8,128)(2,1)S(1)}, u32[]{:S(2)}, u32[]{:S(2)}) collective-permute-start(bf16[8,2,64,128]{3,2,1,0:T(8,128)(2,1)S(1)} %slice_dynamic-update-slice_fusion.refs_0_), channel_id=1, source_target_pairs={{0,4},{1,5},{2,6},{3,7},{4,0},{5,1},{6,2},{7,3},{8,12},{9,13},{10,... | collective-permute-start | bytes 786440 | tf_op jit(solution)/shard_map/ppermute | solution.py:676
  222.3 21.6 %collective-permute-start.17 = (bf16[8,2,64,128]{3,2,1,0:T(8,128)(2,1)S(1)}, bf16[8,2,64,128]{3,2,1,0:T(8,128)(2,1)S(1)}, u32[]{:S(2)}, u32[]{:S(2)}) collective-permute-start(bf16[8,2,64,128]{3,2,1,0:T(8,128)(2,1)S(1)} %slice_dynamic-update-slice_fusion.refs_0_), channel_id=1, source_target_pairs={{0,6},{1,7},{2,4},{3,5},{4,2},{5,3},{6,0},{7,1},{8,14},{9,15},{10,... | collective-permute-start | bytes 786440 | tf_op jit(solution)/shard_map/ppermute | solution.py:676
  243.9 31.2 %all-to-all-start.7 = ((bf16[32,2,64,128]{3,2,1,0:T(8,128)(2,1)}), bf16[32,2,64,128]{3,2,1,0:T(8,128)(2,1)S(1)}, u32[]{:S(2)}, u32[]{:S(2)}) async-start(bf16[32,2,64,128]{3,2,1,0:T(8,128)(2,1)} %shard_map.127), calls=%async_computation.7 | async-start | bytes 2097152 | tf_op jit(solution)/shard_map/all_to_all | solution.py:692
  250.7 24.3 %collective-permute-start.21 = (bf16[16,2,64,128]{3,2,1,0:T(8,128)(2,1)}, bf16[16,2,64,128]{3,2,1,0:T(8,128)(2,1)}, u32[]{:S(2)}, u32[]{:S(2)}) collective-permute-start(bf16[16,2,64,128]{3,2,1,0:T(8,128)(2,1)} %shard_map.131), channel_id=1, source_target_pairs={{0,1},{1,0},{2,3},{3,2},{4,5},{5,4},{6,7},{7,6},{8,9},{9,8},{10,11... | collective-permute-start | bytes 1572872 | tf_op jit(solution)/shard_map/ppermute | solution.py:676
  251.0 17.6 %collective-permute-start.18 = (s16[1056,128]{1,0:T(8,128)(2,1)}, s16[1056,128]{1,0:T(8,128)(2,1)S(1)}, u32[]{:S(2)}, u32[]{:S(2)}) collective-permute-start(s16[1056,128]{1,0:T(8,128)(2,1)} %get-tuple-element.269), channel_id=1, source_target_pairs={{0,2},{1,3},{2,0},{3,1},{4,6},{5,7},{6,4},{7,5},{8,10},{9,11},{10,... | collective-permute-start | bytes 811016 | tf_op jit(solution)/shard_map/ppermute | solution.py:676
  252.6 16.0 %collective-permute-start.19 = (s16[1056,128]{1,0:T(8,128)(2,1)}, s16[1056,128]{1,0:T(8,128)(2,1)S(1)}, u32[]{:S(2)}, u32[]{:S(2)}) collective-permute-start(s16[1056,128]{1,0:T(8,128)(2,1)} %get-tuple-element.270), channel_id=1, source_target_pairs={{0,4},{1,5},{2,6},{3,7},{4,0},{5,1},{6,2},{7,3},{8,12},{9,13},{10,... | collective-permute-start | bytes 811016 | tf_op jit(solution)/shard_map/ppermute | solution.py:676
  253.8 21.3 %collective-permute-start.20 = (s16[1056,128]{1,0:T(8,128)(2,1)S(1)}, s16[1056,128]{1,0:T(8,128)(2,1)S(1)}, u32[]{:S(2)}, u32[]{:S(2)}) collective-permute-start(s16[1056,128]{1,0:T(8,128)(2,1)S(1)} %copy-done.43), channel_id=1, source_target_pairs={{0,6},{1,7},{2,4},{3,5},{4,2},{5,3},{6,0},{7,1},{8,14},{9,15},{10,... | collective-permute-start | bytes 811016 | tf_op jit(solution)/shard_map/ppermute | solution.py:676
  275.1 21.6 %all-to-all-start.8 = ((s16[8,528,128]{2,1,0:T(8,128)(2,1)}), s16[8,528,128]{2,1,0:T(8,128)(2,1)S(1)}, u32[]{:S(2)}, u32[]{:S(2)}) async-start(s16[8,528,128]{2,1,0:T(8,128)(2,1)} %bitcast.37), calls=%async_computation.8 | async-start | bytes 2162688 | tf_op jit(solution)/shard_map/all_to_all | solution.py:695
  296.7 23.3 %all-to-all-start.9 = ((s16[8,528,128]{2,1,0:T(8,128)(2,1)}), s16[8,528,128]{2,1,0:T(8,128)(2,1)S(1)}, u32[]{:S(2)}, u32[]{:S(2)}) async-start(s16[8,528,128]{2,1,0:T(8,128)(2,1)} %bitcast.38), calls=%async_computation.9 | async-start | bytes 2162688 | tf_op jit(solution)/shard_map/all_to_all | solution.py:695
  (54 other events, 402.0 us)
